TPU v7x, 512 devices: a whole 4x8x8 slice. The times are simulated.
512 devices in a mesh: group: 16 (over y, x_hi), dom: 32 (over x_lo, z, core).
Axes of the slice: x: 4 (x_hi: 2, x_lo: 2; x = x_hi * 2 + x_lo), y: 8, z: 8, core: 2. Of those that a mesh axis runs over, the one named last changes fastest.
Arguments:
- slab: float32 [524288, 400], P(('group', 'dom')), may hold values from -3.5 to 3.5
- row_state: float32 [524288], P(('group', 'dom')), may hold values from 0.001 to 0.1
- relation: float32 [8, 400], replicated, may hold values from 0.5 to 1.5
- lhs_rows: int32 [524288], P(('group', 'dom')), may hold values from 0 to 1023
- rhs_rows: int32 [524288], P(('group', 'dom')), may hold values from 0 to 1023
- rel_ids: int32 [524288], P(('group', 'dom')), may hold values from 0 to 7
- neg_start: int32 [4096], P(('group', 'dom')), may hold values from 0 to 512
- live_edges: int32 [512], P(('group', 'dom')), may hold values from 256 to 1024, as said below
Outputs:
- new_slab: float32 [524288, 400], P(('group', 'dom'))
- new_state: float32 [524288], P(('group', 'dom'))
- rel_grad: float32 [8, 400], replicated
Inputs may be any that keep to these rules, and one draw needn't show every extreme that they name: `live_edges`: within 256 to 1024; some partition uses all 1024 slots.
All inputs are finite; a program needn't handle non-finite values.
Results may differ from a plain program's by a relative error of at most 0.0055.
Values may be sent and summed in bfloat16 or wider, within the bound.
No kernel may reach another device: no remote copies, remote signals or barrier semaphores. Data moves between devices by JAX's collectives and lax.ppermute only.
A program may use at most 64 MiB of HBM per device.

v0:
```python
import jax
import jax.numpy as jnp
from jax import lax
from jax.sharding import PartitionSpec as P

BLOCK = 128
NEG = 512
SWAP_BIT = 1


learn_rate = 0.1


def swapped(x, axis, bit):
    return lax.ppermute(x, axis, [(i, i ^ 1 << bit) for i in range(lax.axis_size(axis))])


def block_terms(target_slab, queries, targets, starts, weights):
    blocks = queries.shape[0] // BLOCK
    width = queries.shape[1]

    def step(carry, items):
        query_block, target_block, start, weight_block = items
        negatives = lax.dynamic_slice_in_dim(target_slab, start, NEG, 0)
        positives = target_slab[target_block]
        pos = jnp.sum(query_block.astype(jnp.float32) * positives.astype(jnp.float32), axis=1)
        neg = lax.dot_general(
            query_block, negatives, (((1,), (1,)), ((), ())), preferred_element_type=jnp.float32
        )
        top = jnp.maximum(jnp.max(neg, axis=1), pos)
        pos_exp = jnp.exp(pos - top)
        neg_exp = jnp.exp(neg - top[:, None])
        total = pos_exp + jnp.sum(neg_exp, axis=1)
        gpos = weight_block * (pos_exp / total - 1.0)
        gneg = (weight_block[:, None] * neg_exp / total[:, None]).astype(jnp.bfloat16)
        dquery = gpos[:, None] * positives.astype(jnp.float32) + jnp.dot(
            gneg, negatives, preferred_element_type=jnp.float32
        )
        dneg = lax.dot_general(
            gneg, query_block, (((0,), (0,)), ((), ())), preferred_element_type=jnp.float32
        )
        window = lax.dynamic_slice_in_dim(carry, start, NEG, 0)
        carry = lax.dynamic_update_slice_in_dim(carry, window + dneg, start, 0)
        carry = carry.at[target_block].add(gpos[:, None] * query_block.astype(jnp.float32))
        return (carry, dquery)

    start_grad = jnp.zeros((target_slab.shape[0], width), jnp.float32)
    items = (
        queries.reshape(blocks, BLOCK, width),
        targets.reshape(blocks, BLOCK),
        starts,
        weights.reshape(blocks, BLOCK),
    )
    target_grad, dquery = lax.scan(step, start_grad, items)
    return (dquery.reshape(blocks * BLOCK, width), target_grad)


def on_device(slab, row_state, relation, lhs_rows, rhs_rows, rel_ids, neg_start, live_edges):
    rows_here = slab.shape[0]
    edge_slots = lhs_rows.shape[0]
    embed = slab.astype(jnp.bfloat16)
    onehot = (rel_ids[None, :] == jnp.arange(relation.shape[0], dtype=jnp.int32)[:, None]).astype(
        jnp.float32
    )
    rel_rows = lax.dot_general(
        onehot,
        relation,
        (((0,), (0,)), ((), ())),
        precision=lax.Precision.HIGHEST,
        preferred_element_type=jnp.float32,
    )
    source_vecs = embed[lhs_rows].astype(jnp.float32)
    queries = (source_vecs * rel_rows).astype(jnp.bfloat16)
    other_slab = swapped(embed, "group", SWAP_BIT)
    weights = (jnp.arange(edge_slots, dtype=jnp.int32) < live_edges[0]).astype(jnp.float32)
    dquery, other_grad = block_terms(other_slab, queries, rhs_rows, neg_start, weights)
    mine_grad = swapped(other_grad, "group", SWAP_BIT)
    grad = (
        jnp.zeros((rows_here, slab.shape[1]), jnp.float32).at[lhs_rows].add(dquery * rel_rows)
        + mine_grad
    )
    rel_part = jnp.dot(
        onehot,
        dquery * source_vecs,
        precision=lax.Precision.HIGHEST,
        preferred_element_type=jnp.float32,
    )
    rel_total = lax.psum(rel_part, ("group", "dom"))
    edge_total = edge_slots * lax.axis_size("group") * lax.axis_size("dom")
    rel_grad = rel_total / jnp.sqrt(jnp.float32(edge_total))
    new_state = row_state + jnp.mean(grad * grad, axis=1)
    new_slab = slab - learn_rate * grad / jnp.sqrt(new_state)[:, None]
    return (new_slab, new_state, rel_grad)


def solution(mesh):
    in_specs = (
        P(("group", "dom"), None),
        P(("group", "dom")),
        P(),
        P(("group", "dom")),
        P(("group", "dom")),
        P(("group", "dom")),
        P(("group", "dom")),
        P(("group", "dom")),
    )
    out_specs = (P(("group", "dom"), None), P(("group", "dom")), P())
    return jax.shard_map(
        on_device, mesh=mesh, in_specs=in_specs, out_specs=out_specs, check_vma=False
    )
```

profile of v0, /device:TPU:1, one launch (start us, length us, event | category | flops | bytes accessed | tf_op | source)
XLA Modules:
  0.0 423.0 jit_solution(12459674966798238954)
XLA Ops:
  3.1 4.0 collective-permute-start
  9.2 5.0 %gather_fusion.1 = bf16[1024,400]{1,0:T(8,128)(2,1)} fusion(bf16[1024,400]{1,0:T(8,128)(2,1)S(1)} %copy.46, s32[1024]{0:T(1024)S(1)} %get-tuple-element.172), kind=kCustom, calls=%fused_computation.1 | custom fusion | bytes 1642496 | tf_op jit(solution)/shard_map/gather | solution.py:72
  22.2 241.2 %while.14 = (s32[]{:T(128)}, f32[1024,400]{1,0:T(8,128)S(1)}, f32[8,128,400]{1,0,2:T(8,128)}, s32[8]{0:T(128)}, f32[8,128]{1,0:T(8,128)}, /*index=5*/bf16[8,128,...) while((s32[]{:T(128)}, f32[1024,400]{1,0:T(8,128)S(1)}, ...), condition=%wide.region_5.6_spmd, body=%wide.region_0.5_spmd.sunk | while | flops 158725888 | bytes 20142924 | solution.py:54
  35.0 2.5 convolution_add_fusion.4
  41.9 2.5 scatter_fusion
  45.5 7.0 %dynamic_update_slice.16 = f32[8,128,400]{1,0,2:T(8,128)} dynamic-update-slice(f32[8,128,400]{1,0,2:T(8,128)} %get-tuple-element.245, f32[1,128,400]{1,0,2:T(1,128)} %bitcast.60, s32[]{:T(128)} %get-tuple-element.243, s32[]{:T(128)} %constant.57.clone.1..sunk, s32[]{:T(128)} %constant.57.clone.1..sunk) | dynamic-update-slice | bytes 409604 | tf_op jit(solution)/shard_map/while/body/jit(dynamic_update_index_in_dim)/dynamic_update_slice | solution.py:54
  65.3 2.5 convolution_add_fusion.4
  72.0 2.5 scatter_fusion
  75.7 7.0 %dynamic_update_slice.16 = f32[8,128,400]{1,0,2:T(8,128)} dynamic-update-slice(f32[8,128,400]{1,0,2:T(8,128)} %get-tuple-element.245, f32[1,128,400]{1,0,2:T(1,128)} %bitcast.60, s32[]{:T(128)} %get-tuple-element.243, s32[]{:T(128)} %constant.57.clone.1..sunk, s32[]{:T(128)} %constant.57.clone.1..sunk) | dynamic-update-slice | bytes 409604 | tf_op jit(solution)/shard_map/while/body/jit(dynamic_update_index_in_dim)/dynamic_update_slice | solution.py:54
  95.4 2.5 convolution_add_fusion.4
  102.1 2.5 scatter_fusion
  105.7 7.0 %dynamic_update_slice.16 = f32[8,128,400]{1,0,2:T(8,128)} dynamic-update-slice(f32[8,128,400]{1,0,2:T(8,128)} %get-tuple-element.245, f32[1,128,400]{1,0,2:T(1,128)} %bitcast.60, s32[]{:T(128)} %get-tuple-element.243, s32[]{:T(128)} %constant.57.clone.1..sunk, s32[]{:T(128)} %constant.57.clone.1..sunk) | dynamic-update-slice | bytes 409604 | tf_op jit(solution)/shard_map/while/body/jit(dynamic_update_index_in_dim)/dynamic_update_slice | solution.py:54
  125.5 2.6 convolution_add_fusion.4
  132.3 2.5 scatter_fusion
  136.0 7.0 %dynamic_update_slice.16 = f32[8,128,400]{1,0,2:T(8,128)} dynamic-update-slice(f32[8,128,400]{1,0,2:T(8,128)} %get-tuple-element.245, f32[1,128,400]{1,0,2:T(1,128)} %bitcast.60, s32[]{:T(128)} %get-tuple-element.243, s32[]{:T(128)} %constant.57.clone.1..sunk, s32[]{:T(128)} %constant.57.clone.1..sunk) | dynamic-update-slice | bytes 409604 | tf_op jit(solution)/shard_map/while/body/jit(dynamic_update_index_in_dim)/dynamic_update_slice | solution.py:54
  155.7 2.5 convolution_add_fusion.4
  162.4 2.5 scatter_fusion
  166.1 7.0 %dynamic_update_slice.16 = f32[8,128,400]{1,0,2:T(8,128)} dynamic-update-slice(f32[8,128,400]{1,0,2:T(8,128)} %get-tuple-element.245, f32[1,128,400]{1,0,2:T(1,128)} %bitcast.60, s32[]{:T(128)} %get-tuple-element.243, s32[]{:T(128)} %constant.57.clone.1..sunk, s32[]{:T(128)} %constant.57.clone.1..sunk) | dynamic-update-slice | bytes 409604 | tf_op jit(solution)/shard_map/while/body/jit(dynamic_update_index_in_dim)/dynamic_update_slice | solution.py:54
  185.8 2.5 convolution_add_fusion.4
  196.3 7.0 %dynamic_update_slice.16 = f32[8,128,400]{1,0,2:T(8,128)} dynamic-update-slice(f32[8,128,400]{1,0,2:T(8,128)} %get-tuple-element.245, f32[1,128,400]{1,0,2:T(1,128)} %bitcast.60, s32[]{:T(128)} %get-tuple-element.243, s32[]{:T(128)} %constant.57.clone.1..sunk, s32[]{:T(128)} %constant.57.clone.1..sunk) | dynamic-update-slice | bytes 409604 | tf_op jit(solution)/shard_map/while/body/jit(dynamic_update_index_in_dim)/dynamic_update_slice | solution.py:54
  216.0 2.5 convolution_add_fusion.4
  226.3 7.0 %dynamic_update_slice.16 = f32[8,128,400]{1,0,2:T(8,128)} dynamic-update-slice(f32[8,128,400]{1,0,2:T(8,128)} %get-tuple-element.245, f32[1,128,400]{1,0,2:T(1,128)} %bitcast.60, s32[]{:T(128)} %get-tuple-element.243, s32[]{:T(128)} %constant.57.clone.1..sunk, s32[]{:T(128)} %constant.57.clone.1..sunk) | dynamic-update-slice | bytes 409604 | tf_op jit(solution)/shard_map/while/body/jit(dynamic_update_index_in_dim)/dynamic_update_slice | solution.py:54
  246.1 2.6 convolution_add_fusion.4
  252.8 2.5 scatter_fusion
  256.4 7.0 %dynamic_update_slice.16 = f32[8,128,400]{1,0,2:T(8,128)} dynamic-update-slice(f32[8,128,400]{1,0,2:T(8,128)} %get-tuple-element.245, f32[1,128,400]{1,0,2:T(1,128)} %bitcast.60, s32[]{:T(128)} %get-tuple-element.243, s32[]{:T(128)} %constant.57.clone.1..sunk, s32[]{:T(128)} %constant.57.clone.1..sunk) | dynamic-update-slice | bytes 409604 | tf_op jit(solution)/shard_map/while/body/jit(dynamic_update_index_in_dim)/dynamic_update_slice | solution.py:54
  265.1 3.8 collective-permute-start.1
  268.9 2.9 copy.54
  271.8 3.2 bitcast_multiply_fusion
  275.0 3.0 copy.53
  279.0 127.4 %psum.7 = f32[8,400]{1,0:T(8,128)S(1)} all-reduce(f32[8,400]{1,0:T(8,128)S(1)} %fusion.17), channel_id=1, replica_groups=mesh['group'=16,'dom'=32] {'group','dom'}, use_global_device_ids=true, to_apply=%region_8.9 | all-reduce | flops 3200 | bytes 25600 | tf_op jit(solution)/shard_map/psum | solution.py:88
  408.9 8.0 %scatter_fusion.1 = f32[1024,400]{1,0:T(8,128)S(1)} fusion(f32[1024,400]{1,0:T(8,128)S(1)} %copy.52, s32[1024]{0:T(1024)S(1)} %copy-done.14, f32[1024,400]{1,0:T(8,128)} %copy.53), kind=kCustom, calls=%fused_computation.3 | custom fusion | flops 409600 | bytes 4919296 | tf_op jit(solution)/shard_map/scatter-add | solution.py:79
  420.3 2.7 copy.55
  (253 shorter events, 154.0 us)
Async XLA Ops:
  0.6 16.4 %copy-start = (f32[8,400]{1,0:T(8,128)S(1)}, f32[8,400]{1,0:T(8,128)}, u32[]{:S(2)}) copy-start(f32[8,400]{1,0:T(8,128)} %param.12) | copy-start | bytes 38404
  0.6 8.0 %copy-start.15 = (s32[1024]{0:T(1024)S(1)}, s32[1024]{0:T(1024)}, u32[]{:S(2)}) copy-start(s32[1024]{0:T(1024)} %param.13) | copy-start | bytes 12292
  3.1 17.4 %collective-permute-start = (bf16[1024,400]{0,1:T(8,128)(2,1)}, bf16[1024,400]{0,1:T(8,128)(2,1)}, u32[]{:S(2)}, u32[]{:S(2)}) collective-permute-start(bf16[1024,400]{0,1:T(8,128)(2,1)} %convert_element_type.35), channel_id=1, source_target_pairs={{0,64},{32,96},{64,0},{96,32},{128,192},{160,224},{192,128},{224,1... | collective-permute-start | bytes 2457608 | tf_op jit(solution)/shard_map/ppermute | solution.py:15
  14.3 2.7 copy-start.12
  15.8 3.4 copy-start.7
  22.2 12.8 %copy-start.1 = (bf16[1024,400]{1,0:T(8,128)(2,1)}, bf16[1024,400]{1,0:T(8,128)(2,1)S(1)}, u32[]{:S(2)}) copy-start(bf16[1024,400]{1,0:T(8,128)(2,1)S(1)} %get-tuple-element.260) | copy-start | bytes 2457604 | tf_op jit(solution)/shard_map/while
  39.1 2.8 copy-start.11
  41.9 2.6 copy-start.5
  52.5 12.7 %copy-start.1 = (bf16[1024,400]{1,0:T(8,128)(2,1)}, bf16[1024,400]{1,0:T(8,128)(2,1)S(1)}, u32[]{:S(2)}) copy-start(bf16[1024,400]{1,0:T(8,128)(2,1)S(1)} %get-tuple-element.260) | copy-start | bytes 2457604 | tf_op jit(solution)/shard_map/while
  69.3 2.7 copy-start.11
  72.0 2.6 copy-start.5
  82.6 12.7 %copy-start.1 = (bf16[1024,400]{1,0:T(8,128)(2,1)}, bf16[1024,400]{1,0:T(8,128)(2,1)S(1)}, u32[]{:S(2)}) copy-start(bf16[1024,400]{1,0:T(8,128)(2,1)S(1)} %get-tuple-element.260) | copy-start | bytes 2457604 | tf_op jit(solution)/shard_map/while
  99.4 2.7 copy-start.11
  102.1 2.6 copy-start.5
  112.7 12.7 %copy-start.1 = (bf16[1024,400]{1,0:T(8,128)(2,1)}, bf16[1024,400]{1,0:T(8,128)(2,1)S(1)}, u32[]{:S(2)}) copy-start(bf16[1024,400]{1,0:T(8,128)(2,1)S(1)} %get-tuple-element.260) | copy-start | bytes 2457604 | tf_op jit(solution)/shard_map/while
  129.5 2.8 copy-start.11
  132.3 2.6 copy-start.5
  143.0 12.7 %copy-start.1 = (bf16[1024,400]{1,0:T(8,128)(2,1)}, bf16[1024,400]{1,0:T(8,128)(2,1)S(1)}, u32[]{:S(2)}) copy-start(bf16[1024,400]{1,0:T(8,128)(2,1)S(1)} %get-tuple-element.260) | copy-start | bytes 2457604 | tf_op jit(solution)/shard_map/while
  159.7 2.7 copy-start.11
  162.4 2.6 copy-start.5
  173.1 12.7 %copy-start.1 = (bf16[1024,400]{1,0:T(8,128)(2,1)}, bf16[1024,400]{1,0:T(8,128)(2,1)S(1)}, u32[]{:S(2)}) copy-start(bf16[1024,400]{1,0:T(8,128)(2,1)S(1)} %get-tuple-element.260) | copy-start | bytes 2457604 | tf_op jit(solution)/shard_map/while
  189.8 2.8 copy-start.11
  203.2 12.7 %copy-start.1 = (bf16[1024,400]{1,0:T(8,128)(2,1)}, bf16[1024,400]{1,0:T(8,128)(2,1)S(1)}, u32[]{:S(2)}) copy-start(bf16[1024,400]{1,0:T(8,128)(2,1)S(1)} %get-tuple-element.260) | copy-start | bytes 2457604 | tf_op jit(solution)/shard_map/while
  220.0 2.7 copy-start.11
  233.3 12.7 %copy-start.1 = (bf16[1024,400]{1,0:T(8,128)(2,1)}, bf16[1024,400]{1,0:T(8,128)(2,1)S(1)}, u32[]{:S(2)}) copy-start(bf16[1024,400]{1,0:T(8,128)(2,1)S(1)} %get-tuple-element.260) | copy-start | bytes 2457604 | tf_op jit(solution)/shard_map/while
  250.1 2.7 copy-start.11
  252.8 2.6 copy-start.5
  265.1 6.7 %copy-start.4 = (f32[1024,400]{0,1:T(8,128)S(1)}, f32[1024,400]{0,1:T(8,128)}, u32[]{:S(2)}) copy-start(f32[1024,400]{0,1:T(8,128)} %copy-done.3) | copy-start | bytes 4915204
  265.1 141.9 %collective-permute-start.1 = (f32[1024,400]{0,1:T(8,128)}, f32[1024,400]{0,1:T(8,128)}, u32[]{:S(2)}, u32[]{:S(2)}) collective-permute-start(f32[1024,400]{0,1:T(8,128)} %copy.50), channel_id=1, source_target_pairs={{0,64},{32,96},{64,0},{96,32},{128,192},{160,224},{192,128},{224,1... | collective-permute-start | bytes 4915208 | tf_op jit(solution)/shard_map/ppermute | solution.py:15
  275.0 3.0 copy-start.8
  275.0 3.0 copy-start.9
  275.0 3.0 copy-start.13
  (22 other events, 35.2 us)
where the time goes:
time: 427 us; the launch traced here: 423 us
  local copies, waits for them, and re-layouts  146 us (34%)
  blocking collectives  127 us (30%)
  other arithmetic  77.4 us (18%)
  matrix products  45.5 us (11%)
  loops' own time  16.1 us (4%)
  starting transfers between devices  7.82 us (2%)
    psum x1, blocking collectives, on_device(): rel_total = lax.psum(rel_part, ('group', 'dom'))  127 us
    dynamic_update_slice x8, local copies, waits for them, and re-layouts, block_terms(): target_grad, dquery = lax.scan(step, start_grad, items)  55.9 us
    dot_general x8, matrix products, step(): lax.dot_general(gneg, query_block, (((0,), (0,)), ((), ())), preferred_el...  20.4 us
    scatter-add x8, other arithmetic, step(): carry.at[target_block].add(gpos[:, None] * query_block.astype(jnp.float32))  20.2 us
    another operation x1, loops' own time, block_terms(): target_grad, dquery = lax.scan(step, start_grad, items)  16.1 us
    dot_general x8, matrix products, step(): lax.dot_general(query_block, negatives, (((1,), (1,)), ((), ())), preferr...  14.6 us
    gather x16, local copies, waits for them, and re-layouts, step(): positives = target_slab[target_block]  13.7 us
    another operation x9, local copies, waits for them, and re-layouts  13.7 us
  transfers between devices with their start and end apart: 2, of which 1 were waited for; matrix products, arithmetic and copies ran while one was open for 5% of the time, Pallas kernels for 0%

commit v1 on v0

v1 whole, which is shorter than its diff:
```python
import jax
import jax.numpy as jnp
from jax import lax
from jax.experimental import pallas as pl
from jax.experimental.pallas import tpu as pltpu
from jax.sharding import Mesh
from jax.sharding import PartitionSpec as P

BLOCK = 128
NEG = 512
AXES = ("y", "x_hi", "x_lo", "z", "core")
TILE = 256

learn_rate = 0.1

NN = (((1,), (0,)), ((), ()))
NT = (((1,), (1,)), ((), ()))
TN = (((0,), (0,)), ((), ()))


def swapped(x):
    return lax.ppermute(x, "y", [(i, i ^ 1) for i in range(lax.axis_size("y"))])


def summed(x, axes):
    terms = jnp.broadcast_to(x[None], (lax.axis_size(axes),) + x.shape)
    return jnp.sum(lax.all_to_all(terms, axes, 0, 0), axis=0)


def dot(a, b, dims):
    return lax.dot_general(a, b, dims, preferred_element_type=jnp.float32)


def split(x):
    high = x.astype(jnp.bfloat16)
    return high, (x - high.astype(jnp.float32)).astype(jnp.bfloat16)


def prepare_kernel(
    starts, live, embed, relation, lhs, rhs, kinds, source, rel_rows, query, query_rows, counts, target, target_grad
):
    rows, edges = embed.shape[1], lhs.shape[1]
    kind_hot = lax.broadcasted_iota(jnp.int32, (relation.shape[0], edges), 0) == kinds[...]
    rel_rows[...] = lax.dot_general(
        relation[...],
        kind_hot.astype(jnp.float32),
        TN,
        precision=lax.Precision.HIGHEST,
        preferred_element_type=jnp.float32,
    )
    for at in range(0, edges, TILE):
        here = slice(at, at + TILE)
        left_hot = lax.broadcasted_iota(jnp.int32, (rows, TILE), 0) == lhs[:, here]
        source[:, here] = dot(
            embed[...], left_hot.astype(jnp.float32).astype(jnp.bfloat16), NN
        )
        query_here = source[:, here] * rel_rows[:, here]
        query[:, here] = query_here.astype(jnp.bfloat16)
        query_rows[here, :] = query_here.T.astype(jnp.bfloat16)
    row = lax.broadcasted_iota(jnp.int32, (BLOCK, rows), 1)
    for block in range(edges // BLOCK):
        here = slice(block * BLOCK, (block + 1) * BLOCK)
        index = jnp.broadcast_to(rhs[:, here].astype(jnp.float32), (BLOCK, BLOCK)).T
        index = jnp.concatenate([index] * (rows // BLOCK), axis=1).astype(jnp.int32)
        slot = lax.broadcasted_iota(jnp.int32, (BLOCK, rows), 0) + block * BLOCK
        right_hot = (row == index).astype(jnp.float32)
        begin = starts[block]
        window = ((row >= begin) & (row < begin + NEG)).astype(jnp.float32)
        counts[here, :] = (window + right_hot).astype(jnp.bfloat16)
        target[here, :] = jnp.where(slot < live[0], right_hot, 0.0).astype(jnp.bfloat16)
    target_grad[...] = -dot(query[...], target[...], NN)


def score_kernel(live, other, query, query_rows, counts, target_grad, softmax, sent_grad):
    edges = query.shape[1]
    total_grad = target_grad[...]
    for at in range(0, edges, TILE):
        here = slice(at, at + TILE)
        count = counts[here, :].astype(jnp.float32)
        score = jnp.where(count > 0.0, dot(query_rows[here, :], other[...], NN), -1e30)
        top = jnp.max(score, axis=1, keepdims=True)
        power = jnp.exp(score - top) * count
        total = jnp.sum(power, axis=1, keepdims=True)
        slot = lax.broadcasted_iota(jnp.int32, total.shape, 0) + at
        weight = jnp.where(slot < live[0], 1.0, 0.0) / total
        softmax[here, :] = (power * weight).astype(jnp.bfloat16)
        total_grad = total_grad + dot(query[:, here], softmax[here, :], NN)
    sent_grad[...] = total_grad.astype(jnp.bfloat16)


def relation_kernel(other, softmax, target, source, rel_rows, kinds, rel_part, left_grad):
    edges = kinds.shape[1]
    part = jnp.zeros(rel_part.shape, jnp.float32)
    for at in range(0, edges, TILE):
        here = slice(at, at + TILE)
        dquery = dot(other[...], softmax[here, :], NT) - dot(other[...], target[here, :], NT)
        kind_hot = lax.broadcasted_iota(jnp.int32, (rel_part.shape[0], TILE), 0) == kinds[:, here]
        kind_hot = kind_hot.astype(jnp.float32).astype(jnp.bfloat16)
        high, low = split(dquery * source[:, here])
        part = part + dot(kind_hot, high, NT) + dot(kind_hot, low, NT)
        left_grad[:, here] = (dquery * rel_rows[:, here]).astype(jnp.bfloat16)
    rel_part[...] = part


def update_kernel(slab, state, left_grad, lhs, received, new_slab, new_state):
    rows, edges = slab.shape[1], lhs.shape[1]
    grad = received[...].astype(jnp.float32)
    for at in range(0, edges, TILE):
        here = slice(at, at + TILE)
        left_hot = lax.broadcasted_iota(jnp.int32, (rows, TILE), 0) == lhs[:, here]
        grad = grad + dot(left_grad[:, here], left_hot.astype(jnp.float32).astype(jnp.bfloat16), NT)
    total = state[...] + jnp.sum(grad * grad, axis=0, keepdims=True) * (1.0 / grad.shape[0])
    new_state[...] = total
    new_slab[...] = slab[...] - grad * (learn_rate / jnp.sqrt(total))


def call(kernel, outs, scalars, vectors, flops):
    scalar = pl.BlockSpec(memory_space=pltpu.SMEM)
    vector = pl.BlockSpec(memory_space=pltpu.VMEM)
    return pl.pallas_call(
        kernel,
        out_shape=[jax.ShapeDtypeStruct(shape, dtype) for shape, dtype in outs],
        in_specs=[scalar] * len(scalars) + [vector] * len(vectors),
        out_specs=[vector] * len(outs),
        compiler_params=pltpu.CompilerParams(vmem_limit_bytes=48 * 2**20),
        cost_estimate=pl.CostEstimate(flops=flops, bytes_accessed=8 * 2**20, transcendentals=0),
    )(*scalars, *vectors)


def on_device(slab, row_state, relation, lhs_rows, rhs_rows, rel_ids, neg_start, live_edges):
    rows, width = slab.shape
    edges = lhs_rows.shape[0]
    bf16, f32 = jnp.bfloat16, jnp.float32
    columns = slab.T
    embed = columns.astype(bf16)
    other = swapped(embed)
    lhs, rhs, kinds = (x.reshape(1, edges) for x in (lhs_rows, rhs_rows, rel_ids))
    work = 2 * rows * edges * width
    source, rel_rows, query, query_rows, counts, target, target_grad = call(
        prepare_kernel,
        [
            ((width, edges), f32),
            ((width, edges), f32),
            ((width, edges), bf16),
            ((edges, width), bf16),
            ((edges, rows), bf16),
            ((edges, rows), bf16),
            ((width, rows), f32),
        ],
        (neg_start, live_edges),
        (embed, relation, lhs, rhs, kinds),
        2 * work,
    )
    softmax, sent_grad = call(
        score_kernel,
        [((edges, rows), bf16), ((width, rows), bf16)],
        (live_edges,),
        (other, query, query_rows, counts, target_grad),
        2 * work,
    )
    received = swapped(sent_grad)
    rel_part, left_grad = call(
        relation_kernel,
        [(relation.shape, f32), ((width, edges), bf16)],
        (),
        (other, softmax, target, source, rel_rows, kinds),
        3 * work,
    )
    rel_total = summed(summed(summed(rel_part, ("z", "core")), ("x_hi", "x_lo")), "y")
    edge_total = edges * lax.axis_size(AXES)
    rel_grad = rel_total / jnp.sqrt(jnp.float32(edge_total))
    new_columns, new_state = call(
        update_kernel,
        [((width, rows), f32), ((1, rows), f32)],
        (),
        (columns, row_state.reshape(1, rows), left_grad, lhs, received),
        work,
    )
    return (new_columns.T, new_state.reshape(rows), rel_grad)


def solution(mesh):
    group, dom = mesh.devices.shape
    fine = Mesh(mesh.devices.reshape(group // 2, 2, 2, dom // 4, 2), AXES)
    split_rows, split = P(AXES, None), P(AXES)
    in_specs = (split_rows, split, P(), split, split, split, split, split)
    out_specs = (split_rows, split, P())
    return jax.shard_map(
        on_device, mesh=fine, in_specs=in_specs, out_specs=out_specs, check_vma=False
    )
```

time: 427 us -> 90.5 us (0.21)
  local copies, waits for them, and re-layouts: 146 us -> 3.81 us
  blocking collectives: 127 us -> 23 us
  other arithmetic: 77.4 us -> 2.83 us
  matrix products: 45.5 us -> 0 us
  Pallas kernels: 0 us -> 20.5 us
  loops' own time: 16.1 us -> 0 us
  starting transfers between devices: 7.82 us -> 23.9 us
  waiting for transfers between devices: 1.18 us -> 14.6 us
    psum x1 -> x0, blocking collectives: 127 us -> none  [on_device(): rel_total = lax.psum(rel_part, ('group', 'dom'))]
    dynamic_update_slice x16 -> x0, local copies, waits for them, and re-layouts: 63.7 us -> none  [the longest x8 55.9 us: block_terms(): target_grad, dquery = lax.scan(step, start_grad, items)]
    dot_general x26 -> x0, matrix products: 45.5 us -> none  [the longest x8 20.4 us: step(): lax.dot_general(gneg, query_block, (((0,), (0,)), ((), ())), preferred_el...]
    scatter-add x9 -> x0, other arithmetic: 28.3 us -> none  [the longest x8 20.2 us: step(): carry.at[target_block].add(gpos[:, None] * query_block.astype(jnp.float32))]
    all_to_all x0 -> x2, blocking collectives: none -> 23 us  [summed(): return jnp.sum(lax.all_to_all(terms, axes, 0, 0), axis=0)]
    pallas_call x0 -> x4, Pallas kernels: none -> 20.5 us  [call(): pl.pallas_call(kernel, out_shape=[jax.ShapeDtypeStruct(shape, dtype) for...]
    gather x18 -> x0, local copies, waits for them, and re-layouts: 20.2 us -> none  [the longest x16 13.7 us: step(): positives = target_slab[target_block]]
    all_to_all x0 -> x1, starting transfers between devices: none -> 16.6 us  [summed(): return jnp.sum(lax.all_to_all(terms, axes, 0, 0), axis=0)]
  transfers between devices with their start and end apart: 2 -> 3, of which waited for: 1 -> 2; matrix products, arithmetic and copies ran while one was open for 5% -> 2% of each run, Pallas kernels for 0% -> 7%
where the time goes in v1:
time: 90.5 us; the launch traced here: 90 us
  starting transfers between devices  23.9 us (26%)
  blocking collectives  23 us (25%)
  Pallas kernels  20.5 us (23%)
  waiting for transfers between devices  14.6 us (16%)
  local copies, waits for them, and re-layouts  3.81 us (4%)
  other arithmetic  2.83 us (3%)
  between operations  1.42 us (2%)
    all_to_all x2, blocking collectives, summed(): return jnp.sum(lax.all_to_all(terms, axes, 0, 0), axis=0)  23 us
    pallas_call x4, Pallas kernels, call(): pl.pallas_call(kernel, out_shape=[jax.ShapeDtypeStruct(shape, dtype) for...  20.5 us
    all_to_all x1, starting transfers between devices, summed(): return jnp.sum(lax.all_to_all(terms, axes, 0, 0), axis=0)  16.6 us
    all_to_all x1, waiting for transfers between devices, summed(): return jnp.sum(lax.all_to_all(terms, axes, 0, 0), axis=0)  8.48 us
    ppermute x2, starting transfers between devices, swapped(): return lax.ppermute(x, 'y', [(i, i ^ 1) for i in range(lax.axis_size('y'))])  7.26 us
    ppermute x2, waiting for transfers between devices, swapped(): return lax.ppermute(x, 'y', [(i, i ^ 1) for i in range(lax.axis_size('y'))])  6.12 us
    unnamed x18, local copies, waits for them, and re-layouts  2.36 us
  transfers between devices with their start and end apart: 3, of which 2 were waited for; matrix products, arithmetic and copies ran while one was open for 2% of the time, Pallas kernels for 7%

profile of v1, /device:TPU:1, one launch (start us, length us, event | category | flops | bytes accessed | tf_op | source)
XLA Modules:
  0.0 90.0 jit_solution(16227862401135512265)
XLA Ops:
  0.6 0.0 copy-start.8
  0.6 0.0 copy-start.7
  0.7 0.0 copy-start.6
  0.7 0.0 copy-start.3
  0.7 0.0 copy-start.5
  0.7 1.6 %bitcast_convert_fusion.embed = bf16[400,1024]{1,0:T(8,128)(2,1)S(1)} fusion(f32[1024,400]{0,1:T(8,128)} %param.8), kind=kLoop, calls=%fused_computation.1 | loop fusion | flops 409600 | bytes 2457600 | tf_op jit(solution)/shard_map/convert_element_type | solution.py:135
  2.3 4.0 %collective-permute-start = (bf16[400,1024]{1,0:T(8,128)(2,1)S(1)}, bf16[400,1024]{1,0:T(8,128)(2,1)S(1)}, u32[]{:S(2)}, u32[]{:S(2)}) collective-permute-start(bf16[400,1024]{1,0:T(8,128)(2,1)S(1)} %bitcast_convert_fusion.embed), channel_id=1, source_target_pairs={{0,64},{64,0},{128,192},{192,128},{256,320},{320,256},{384,448},{4... | collective-permute-start | bytes 2457608 | tf_op jit(solution)/shard_map/ppermute | solution.py:22
  7.0 0.0 copy-done.8
  7.0 0.0 copy-done.7
  7.0 0.0 copy-done.6
  7.0 0.0 copy-done.3
  7.0 0.0 copy-done.5
  7.0 6.2 %shard_map.103 = (f32[400,1024]{1,0:T(8,128)S(1)}, f32[400,1024]{1,0:T(8,128)S(1)}, bf16[400,1024]{1,0:T(8,128)(2,1)S(1)}, bf16[1024,400]{1,0:T(8,128)(2,1)S(1)}...) custom-call(s32[8]{0:T(128)S(1)} %copy-done.8, s32[1]{0:T(128)S(6)} %copy.11.live, ...), custom_call_target="tpu_custom_call" | custom-call | flops 1677721600 | bytes 8388608 | tf_op jit(solution)/shard_map/pallas_call | solution.py:120
  13.2 6.1 %collective-permute-done.other = bf16[400,1024]{1,0:T(8,128)(2,1)S(1)} collective-permute-done((bf16[400,1024]{1,0:T(8,128)(2,1)S(1)}, bf16[400,1024]{1,0:T(8,128)(2,1)S(1)}, u32[]{:S(2)}, u32[]{:S(2)}) %collective-permute-start) | collective-permute-done | bytes 819232 | tf_op jit(solution)/shard_map/ppermute | solution.py:22
  19.3 1.4 %copy-done.1 = f32[400,1024]{1,0:T(8,128)S(1)} copy-done((f32[400,1024]{1,0:T(8,128)S(1)}, f32[400,1024]{1,0:T(8,128)}, u32[]{:S(2)}) %copy-start.1) | copy-done | bytes 1638424
  20.8 6.6 %shard_map.104 = (bf16[1024,1024]{1,0:T(8,128)(2,1)}, bf16[400,1024]{1,0:T(8,128)(2,1)S(1)}) custom-call(s32[1]{0:T(128)S(6)} %copy.11.live, bf16[400,1024]{1,0:T(8,128)(2,1)S(1)} %collective-permute-done.other, bf16[400,1024]{1,0:T(8,128)(2,1)S(1)} %get-tuple-element.16.query, bf16[1024,400]{1,0:T(8,128)(2,1)S(1)} %get-tuple-element.17.query_rows, ...), custom_call_target="tpu_custom_call" | custom-call | flops 1677721600 | bytes 8388608 | tf_op jit(solution)/shard_map/pallas_call | solution.py:120
  27.4 0.9 copy-done.4
  28.3 5.0 %shard_map.105 = (f32[8,400]{1,0:T(8,128)S(1)}, bf16[400,1024]{1,0:T(8,128)(2,1)S(1)}) custom-call(bf16[400,1024]{1,0:T(8,128)(2,1)S(1)} %collective-permute-done.other, bf16[1024,1024]{1,0:T(8,128)(2,1)} %get-tuple-element.20.softmax, bf16[1024,1024]{1,0:T(8,128)(2,1)} %get-tuple-element.21.target, f32[400,1024]{1,0:T(8,128)S(1)} %get-tuple-element.22.source, ...), custom_call_target="tpu_custom_call" | custom-call | flops 2516582400 | bytes 8388608 | tf_op jit(solution)/shard_map/pallas_call | solution.py:120
  33.3 0.0 copy-start.2
  33.3 0.7 broadcast_in_dim.6
  34.1 16.6 %all-to-all-start = ((f32[16,8,400]{2,1,0:T(8,128)}), f32[16,8,400]{2,1,0:T(8,128)S(1)}, u32[]{:S(2)}, u32[]{:S(2)}) async-start(f32[16,8,400]{2,1,0:T(8,128)} %broadcast_in_dim.6), calls=%async_computation | async-start | bytes 524288 | tf_op jit(solution)/shard_map/all_to_all | solution.py:27
  50.7 3.2 %collective-permute-start.1 = (bf16[400,1024]{1,0:T(8,128)(2,1)}, bf16[400,1024]{1,0:T(8,128)(2,1)S(1)}, u32[]{:S(2)}, u32[]{:S(2)}) collective-permute-start(bf16[400,1024]{1,0:T(8,128)(2,1)} %copy-done.4), channel_id=1, source_target_pairs={{0,64},{64,0},{128,192},{192,128},{256,320},{320,256},{384,448},{4... | collective-permute-start | bytes 2457608 | tf_op jit(solution)/shard_map/ppermute | solution.py:22
  53.9 8.5 %all-to-all-done = f32[16,8,400]{2,1,0:T(8,128)S(1)} async-done(((f32[16,8,400]{2,1,0:T(8,128)}), f32[16,8,400]{2,1,0:T(8,128)S(1)}, u32[]{:S(2)}, u32[]{:S(2)}) %all-to-all-start) | async-done | bytes 204832 | tf_op jit(solution)/shard_map/all_to_all | solution.py:27
  62.4 0.6 reduce_sum.27
  63.0 0.7 broadcast_in_dim.7
  63.8 8.3 %all_to_all.15 = f32[4,8,400]{2,1,0:T(8,128)S(1)} all-to-all(f32[4,8,400]{2,1,0:T(8,128)S(1)} %broadcast_in_dim.7), channel_id=1, replica_groups=mesh['y'=8,'x_hi'=2,'x_lo'=2,'z'=8,'core'=2] {'x_hi','x_lo'}, dimensions={0} | all-to-all | bytes 102400 | tf_op jit(solution)/shard_map/all_to_all | solution.py:27
  72.1 14.7 %all_to_all.16 = f32[8,8,400]{2,1,0:T(8,128)S(1)} all-to-all(f32[8,8,400]{2,1,0:T(8,128)S(1)} %broadcast_in_dim.8), channel_id=1, replica_groups=mesh['y'=8,'x_hi'=2,'x_lo'=2,'z'=8,'core'=2] {'y'}, dimensions={0} | all-to-all | bytes 204800 | tf_op jit(solution)/shard_map/all_to_all | solution.py:27
  86.8 0.6 broadcast_multiply_fusion
  87.4 0.0 collective-permute-done.1.received
  87.4 0.0 copy-done
  87.4 0.0 copy-done.2
  87.4 2.6 %shard_map.106 = (f32[400,1024]{1,0:T(8,128)}, f32[1,1024]{1,0:T(1,128)}) custom-call(f32[400,1024]{1,0:T(8,128)S(1)} %bitcast.8, f32[1,1024]{1,0:T(1,128)S(1)} %bitcast.9, bf16[400,1024]{1,0:T(8,128)(2,1)S(1)} %get-tuple-element.24.left_grad, s32[1,1024]{1,0:T(1,128)S(1)} %bitcast.11, bf16[400,1024]{1,0:T(8,128)(2,1)S(1)} %collective-permute-done.1.received), custom_call_target="tpu_custom_call" | custom-call | flops 838860800 | bytes 8388608 | tf_op jit(solution)/shard_map/pallas_call | solution.py:120
  (6 shorter events, 0.0 us)
Async XLA Ops:
  0.6 6.3 %copy-start.8 = (s32[8]{0:T(128)S(1)}, s32[8]{0:T(128)}, u32[]{:S(2)}) copy-start(s32[8]{0:T(128)} %starts.1) | copy-start | bytes 100
  0.6 6.3 %copy-start.7 = (s32[1024]{0:T(1024)S(1)}, s32[1024]{0:T(1024)}, u32[]{:S(2)}) copy-start(s32[1024]{0:T(1024)} %param.13) | copy-start | bytes 12292
  0.7 6.3 %copy-start.6 = (s32[1024]{0:T(1024)S(1)}, s32[1024]{0:T(1024)}, u32[]{:S(2)}) copy-start(s32[1024]{0:T(1024)} %param.12) | copy-start | bytes 12292
  0.7 6.3 %copy-start.3 = (s32[1024]{0:T(1024)S(1)}, s32[1024]{0:T(1024)}, u32[]{:S(2)}) copy-start(s32[1024]{0:T(1024)} %param.11) | copy-start | bytes 12292
  0.7 6.3 %copy-start.5 = (f32[8,400]{1,0:T(8,128)S(1)}, f32[8,400]{1,0:T(8,128)}, u32[]{:S(2)}) copy-start(f32[8,400]{1,0:T(8,128)} %relation.1) | copy-start | bytes 38404
  2.3 17.1 %collective-permute-start = (bf16[400,1024]{1,0:T(8,128)(2,1)S(1)}, bf16[400,1024]{1,0:T(8,128)(2,1)S(1)}, u32[]{:S(2)}, u32[]{:S(2)}) collective-permute-start(bf16[400,1024]{1,0:T(8,128)(2,1)S(1)} %bitcast_convert_fusion.embed), channel_id=1, source_target_pairs={{0,64},{64,0},{128,192},{192,128},{256,320},{320,256},{384,448},{4... | collective-permute-start | bytes 2457608 | tf_op jit(solution)/shard_map/ppermute | solution.py:22
  19.3 1.4 %copy-start.1 = (f32[400,1024]{1,0:T(8,128)S(1)}, f32[400,1024]{1,0:T(8,128)}, u32[]{:S(2)}) copy-start(f32[400,1024]{1,0:T(8,128)} %get-tuple-element.19.target_grad) | copy-start | bytes 4915204
  27.4 0.9 copy-start.4
  33.3 54.1 %copy-start = (f32[1024,400]{0,1:T(8,128)S(1)}, f32[1024,400]{0,1:T(8,128)}, u32[]{:S(2)}) copy-start(f32[1024,400]{0,1:T(8,128)} %param.8) | copy-start | bytes 4915204
  33.3 54.1 %copy-start.2 = (f32[1024]{0:T(1024)S(1)}, f32[1024]{0:T(1024)}, u32[]{:S(2)}) copy-start(f32[1024]{0:T(1024)} %param.9) | copy-start | bytes 12292
  34.1 28.3 %all-to-all-start = ((f32[16,8,400]{2,1,0:T(8,128)}), f32[16,8,400]{2,1,0:T(8,128)S(1)}, u32[]{:S(2)}, u32[]{:S(2)}) async-start(f32[16,8,400]{2,1,0:T(8,128)} %broadcast_in_dim.6), calls=%async_computation | async-start | bytes 524288 | tf_op jit(solution)/shard_map/all_to_all | solution.py:27
  50.7 36.7 %collective-permute-start.1 = (bf16[400,1024]{1,0:T(8,128)(2,1)}, bf16[400,1024]{1,0:T(8,128)(2,1)S(1)}, u32[]{:S(2)}, u32[]{:S(2)}) collective-permute-start(bf16[400,1024]{1,0:T(8,128)(2,1)} %copy-done.4), channel_id=1, source_target_pairs={{0,64},{64,0},{128,192},{192,128},{256,320},{320,256},{384,448},{4... | collective-permute-start | bytes 2457608 | tf_op jit(solution)/shard_map/ppermute | solution.py:22

commit v2 on v1

v2 whole, which is shorter than its diff:
```python
import functools
import math

import jax
import jax.numpy as jnp
import numpy as np
from jax import lax
from jax.experimental import pallas as pl
from jax.experimental.pallas import tpu as pltpu
from jax.sharding import Mesh
from jax.sharding import PartitionSpec as P

BLOCK = 128
NEG = 512
AXES = ("y", "x_hi", "x_lo", "z", "core")
NEAR = ("x_hi", "x_lo", "z", "core")
FAR = ("y", "x_lo", "core")
PIECE = 128
TILE = 256
WIDE = 512
CUT = 512
LOG_TWO = 0.6931471805599453
NEVER = -1e30

learn_rate = 0.1

NN = (((1,), (0,)), ((), ()))
NT = (((1,), (1,)), ((), ()))
TN = (((0,), (0,)), ((), ()))


def axis_size(axes):
    return lax.axis_size(axes)


def swapped(x):
    return lax.ppermute(x, "y", [(i, i ^ 1) for i in range(lax.axis_size("y"))])


def exchanged(terms, axes):
    return lax.all_to_all(terms, axes, 0, 0)


def pieces(axes):
    place = np.indices([axis_size(axis) for axis in axes]).reshape(len(axes), -1)
    return [int(k) for k in place[axes.index("x_lo")] * 2 + place[axes.index("core")]]


def dot(a, b, dims):
    return lax.dot_general(a, b, dims, preferred_element_type=jnp.float32)


def split(x):
    high = x.astype(jnp.bfloat16)
    return high, (x - high.astype(jnp.float32)).astype(jnp.bfloat16)


def one_hot(index, classes):
    row = lax.broadcasted_iota(jnp.int32, (classes, index.shape[1]), 0)
    return (row == index).astype(jnp.float32)


def prepare_kernel(starts, live, embed, relation, lhs, rhs, kinds, source, rel_rows, query, query_rows, bias, target, target_grad):
    rows, edges = embed.shape[1], lhs.shape[1]
    rel_rows[...] = lax.dot_general(
        relation[...],
        one_hot(kinds[...], relation.shape[0]),
        TN,
        precision=lax.Precision.HIGHEST,
        preferred_element_type=jnp.float32,
    )
    for at in range(0, edges, TILE):
        here = slice(at, at + TILE)
        source_here = dot(embed[...], one_hot(lhs[:, here], rows).astype(jnp.bfloat16), NN)
        query_here = source_here * rel_rows[:, here]
        source[:, here] = source_here.astype(jnp.bfloat16)
        query[:, here] = query_here.astype(jnp.bfloat16)
        query_rows[here, :] = query_here.T.astype(jnp.bfloat16)
    row = lax.broadcasted_iota(jnp.int32, (BLOCK, rows), 1)
    for block in range(edges // BLOCK):
        here = slice(block * BLOCK, (block + 1) * BLOCK)
        index = jnp.broadcast_to(rhs[:, here].astype(jnp.float32), (BLOCK, BLOCK)).T
        index = jnp.concatenate([index] * (rows // BLOCK), axis=1).astype(jnp.int32)
        slot = lax.broadcasted_iota(jnp.int32, (BLOCK, rows), 0) + block * BLOCK
        is_target = row == index
        begin = starts[block]
        in_window = (row >= begin) & (row < begin + NEG)
        bias[here, :] = jnp.where(
            in_window, jnp.where(is_target, LOG_TWO, 0.0), jnp.where(is_target, 0.0, NEVER)
        )
        target[here, :] = jnp.where(is_target & (slot < live[0]), 1.0, 0.0).astype(jnp.bfloat16)
    target_grad[...] = -dot(query[...], target[...], NN)


def first_kernel(other, query_rows, bias, target, power, top, total, positives):
    edges, cut = bias.shape[0], other.shape[1]
    for at in range(0, edges, TILE):
        here = slice(at, at + TILE)
        score = dot(query_rows[here, :], other[...], NN) + bias[here, :cut]
        top_here = jnp.max(score, axis=1, keepdims=True)
        power_here = jnp.exp(score - top_here)
        power[here, :] = power_here
        top[here, :] = top_here
        total[here, :] = jnp.sum(power_here, axis=1, keepdims=True)
        positives[:, here] = dot(other[...], target[here, :cut], NT)


def second_kernel(
    live, rest, query, query_rows, bias, target_grad, power, top, total, softmax, sent_grad
):
    edges, cut = power.shape
    for at in range(0, edges, TILE):
        here = slice(at, at + TILE)
        score = dot(query_rows[here, :], rest[...], NN) + bias[here, cut:]
        top_here = jnp.maximum(jnp.max(score, axis=1, keepdims=True), top[here, :])
        power_here = jnp.exp(score - top_here)
        scale = jnp.exp(top[here, :] - top_here)
        total_here = jnp.sum(power_here, axis=1, keepdims=True) + total[here, :] * scale
        slot = lax.broadcasted_iota(jnp.int32, total_here.shape, 0) + at
        weight = jnp.where(slot < live[0], 1.0, 0.0) / total_here
        softmax[here, :cut] = (power[here, :] * (scale * weight)).astype(jnp.bfloat16)
        softmax[here, cut:] = (power_here * weight).astype(jnp.bfloat16)
    sent_grad[...] = (target_grad[...] + dot(query[...], softmax[...], NN)).astype(jnp.bfloat16)


def relation_kernel(
    near_pieces, other, rest, softmax, target, positives, source, rel_rows, kinds, left_grad, terms
):
    edges, cut = softmax.shape[0], other.shape[1]
    part = jnp.zeros((source.shape[0], terms.shape[1]), jnp.float32)
    for at in range(0, edges, WIDE):
        here = slice(at, at + WIDE)
        dquery = (
            dot(other[...], softmax[here, :cut], NT)
            + dot(rest[...], softmax[here, cut:], NT)
            - dot(rest[...], target[here, cut:], NT)
            - positives[:, here]
        )
        kind_hot = one_hot(kinds[:, here], part.shape[1]).astype(jnp.bfloat16)
        high, low = split(dquery * source[:, here].astype(jnp.float32))
        part = part + (dot(high, kind_hot, NT) + dot(low, kind_hot, NT))
        left_grad[:, here] = (dquery * rel_rows[:, here]).astype(jnp.bfloat16)
    part = part.T
    part = jnp.concatenate([part, jnp.zeros((part.shape[0], -part.shape[1] % PIECE), part.dtype)], axis=1)
    part = part.astype(terms.dtype)
    for k, piece in enumerate(near_pieces):
        terms[k] = part[:, piece * PIECE : (piece + 1) * PIECE]


def pass_on_kernel(terms, summed):
    total = terms[0].astype(jnp.float32)
    for k in range(1, terms.shape[0]):
        total = total + terms[k].astype(jnp.float32)
    total = total.astype(summed.dtype)
    for k in range(summed.shape[0]):
        summed[k] = total


def collect_kernel(far_pieces, scale, terms, rel_grad):
    width = rel_grad.shape[1]
    total = {}
    for k, piece in enumerate(far_pieces):
        term = terms[k].astype(jnp.float32)
        total[piece] = total[piece] + term if piece in total else term
    for piece, term in total.items():
        end = min(width, (piece + 1) * PIECE)
        rel_grad[:, piece * PIECE : end] = term[:, : end - piece * PIECE] * scale


def source_kernel(left_grad, lhs, source_grad):
    edges, rows = lhs.shape[1], source_grad.shape[1]
    grad = jnp.zeros(source_grad.shape, jnp.float32)
    for at in range(0, edges, TILE):
        here = slice(at, at + TILE)
        grad = grad + dot(left_grad[:, here], one_hot(lhs[:, here], rows).astype(jnp.bfloat16), NT)
    source_grad[...] = grad


def update_kernel(slab, state, source_grad, received, new_slab, new_state):
    grad = source_grad[...] + received[...].astype(jnp.float32)
    total = state[...] + jnp.sum(grad * grad, axis=0, keepdims=True) * (1.0 / grad.shape[0])
    new_state[...] = total
    new_slab[...] = slab[...] - grad * (learn_rate / jnp.sqrt(total))


def call(kernel, outs, scalars, vectors, flops, scratch=()):
    scalar = pl.BlockSpec(memory_space=pltpu.SMEM)
    vector = pl.BlockSpec(memory_space=pltpu.VMEM)
    return pl.pallas_call(
        kernel,
        out_shape=[jax.ShapeDtypeStruct(shape, dtype) for shape, dtype in outs],
        in_specs=[scalar] * len(scalars) + [vector] * len(vectors),
        out_specs=[vector] * len(outs),
        scratch_shapes=[pltpu.VMEM(shape, dtype) for shape, dtype in scratch],
        compiler_params=pltpu.CompilerParams(vmem_limit_bytes=24 * 2**20),
        cost_estimate=pl.CostEstimate(flops=flops, bytes_accessed=8 * 2**20, transcendentals=0),
    )(*scalars, *vectors)


def on_device(slab, row_state, relation, lhs_rows, rhs_rows, rel_ids, neg_start, live_edges):
    rows, width = slab.shape
    edges = lhs_rows.shape[0]
    bf16, f32 = jnp.bfloat16, jnp.float32
    columns = slab.T
    embed = columns.astype(bf16)
    other, rest = swapped(embed[:, :CUT]), swapped(embed[:, CUT:])
    lhs, rhs, kinds = (x.reshape(1, edges) for x in (lhs_rows, rhs_rows, rel_ids))
    work = 2 * rows * edges * width
    source, rel_rows, query, query_rows, bias, target, target_grad = call(
        prepare_kernel,
        [
            ((width, edges), bf16),
            ((width, edges), f32),
            ((width, edges), bf16),
            ((edges, width), bf16),
            ((edges, rows), f32),
            ((edges, rows), bf16),
            ((width, rows), f32),
        ],
        (neg_start, live_edges),
        (embed, relation, lhs, rhs, kinds),
        2 * work,
    )
    power, top, total, positives = call(
        first_kernel,
        [((edges, CUT), f32), ((edges, 1), f32), ((edges, 1), f32), ((width, edges), f32)],
        (),
        (other, query_rows, bias, target),
        work,
    )
    softmax, sent_grad = call(
        second_kernel,
        [((edges, rows), bf16), ((width, rows), bf16)],
        (live_edges,),
        (rest, query, query_rows, bias, target_grad, power, top, total),
        2 * work,
    )
    received = swapped(sent_grad)
    near, far = pieces(NEAR), pieces(FAR)
    piece = (relation.shape[0], PIECE)
    left_grad, terms = call(
        functools.partial(relation_kernel, near),
        [((width, edges), bf16), ((len(near),) + piece, bf16)],
        (),
        (other, rest, softmax, target, positives, source, rel_rows, kinds),
        2 * work,
    )
    terms = exchanged(terms, NEAR)
    (source_grad,) = call(
        source_kernel,
        [((width, rows), f32)],
        (),
        (left_grad, lhs),
        work,
    )
    (terms,) = call(pass_on_kernel, [((len(far),) + piece, bf16)], (), (terms,), 10**5)
    received, terms = lax.optimization_barrier((received, terms))
    terms = exchanged(terms, FAR)
    new_columns, new_state = call(
        update_kernel,
        [((width, rows), f32), ((1, rows), f32)],
        (),
        (columns, row_state.reshape(1, rows), source_grad, received),
        work // 100,
    )
    new_state, terms = lax.optimization_barrier((new_state, terms))
    scale = 1.0 / math.sqrt(edges * axis_size(AXES))
    (rel_grad,) = call(
        functools.partial(collect_kernel, far, scale), [(relation.shape, f32)], (), (terms,), 10**5
    )
    return (new_columns.T, new_state.reshape(rows), rel_grad)


def solution(mesh):
    group, dom = mesh.devices.shape
    fine = Mesh(mesh.devices.reshape(group // 2, 2, 2, dom // 4, 2), AXES)
    split_rows, split = P(AXES, None), P(AXES)
    in_specs = (split_rows, split, P(), split, split, split, split, split)
    out_specs = (split_rows, split, P())
    return jax.shard_map(
        on_device, mesh=fine, in_specs=in_specs, out_specs=out_specs, check_vma=False
    )
```

time: 90.5 us -> 74.6 us (0.82)
  starting transfers between devices: 23.9 us -> 17.1 us
  blocking collectives: 23 us -> 29.2 us
  Pallas kernels: 20.5 us -> 15.1 us
  waiting for transfers between devices: 14.6 us -> 9.83 us
  local copies, waits for them, and re-layouts: 3.81 us -> 0.09 us
  other arithmetic: 2.83 us -> 1.58 us
    all_to_all x1, starting transfers between devices: 16.6 us -> 6.99 us  [exchanged(): return lax.all_to_all(terms, axes, 0, 0)]
    all_to_all x2 -> x1, blocking collectives: 23 us -> 29.2 us  [exchanged(): return lax.all_to_all(terms, axes, 0, 0)]
    pallas_call x4 -> x8, Pallas kernels: 20.5 us -> 15.1 us  [call(): pl.pallas_call(kernel, out_shape=[jax.ShapeDtypeStruct(shape, dtype) for...]
    all_to_all x1, waiting for transfers between devices: 8.48 us -> 5.52 us  [exchanged(): return lax.all_to_all(terms, axes, 0, 0)]
    ppermute x2 -> x3, starting transfers between devices: 7.26 us -> 10.1 us  [swapped(): return lax.ppermute(x, 'y', [(i, i ^ 1) for i in range(lax.axis_size('y'))])]
    unnamed x18 -> x14, local copies, waits for them, and re-layouts: 2.36 us -> 0.03 us
    ppermute x2 -> x3, waiting for transfers between devices: 6.12 us -> 4.3 us  [swapped(): return lax.ppermute(x, 'y', [(i, i ^ 1) for i in range(lax.axis_size('y'))])]
    broadcast_in_dim x3 -> x0, local copies, waits for them, and re-layouts: 1.45 us -> none  [summed(): terms = jnp.broadcast_to(x[None], (lax.axis_size(axes),) + x.shape)]
  transfers between devices with their start and end apart: 3 -> 4, of which waited for: 2 -> 2; matrix products, arithmetic and copies ran while one was open for 2% -> 0% of each run, Pallas kernels for 7% -> 16%
where the time goes in v2:
time: 74.6 us; the launch traced here: 74.3 us
  blocking collectives  29.2 us (39%)
  starting transfers between devices  17.1 us (23%)
  Pallas kernels  15.1 us (20%)
  waiting for transfers between devices  9.83 us (13%)
  other arithmetic  1.58 us (2%)
  between operations  1.46 us (2%)
    all_to_all x1, blocking collectives, exchanged(): return lax.all_to_all(terms, axes, 0, 0)  29.2 us
    pallas_call x8, Pallas kernels, call(): pl.pallas_call(kernel, out_shape=[jax.ShapeDtypeStruct(shape, dtype) for...  15.1 us
    ppermute x3, starting transfers between devices, swapped(): return lax.ppermute(x, 'y', [(i, i ^ 1) for i in range(lax.axis_size('y'))])  10.1 us
    all_to_all x1, starting transfers between devices, exchanged(): return lax.all_to_all(terms, axes, 0, 0)  6.99 us
    all_to_all x1, waiting for transfers between devices, exchanged(): return lax.all_to_all(terms, axes, 0, 0)  5.52 us
    ppermute x3, waiting for transfers between devices, swapped(): return lax.ppermute(x, 'y', [(i, i ^ 1) for i in range(lax.axis_size('y'))])  4.3 us
    convert_element_type x1, other arithmetic, on_device(): embed = columns.astype(bf16)  1.58 us
  transfers between devices with their start and end apart: 4, of which 2 were waited for; matrix products, arithmetic and copies ran while one was open for 0% of the time, Pallas kernels for 16%

profile of v2, /device:TPU:1, one launch (start us, length us, event | category | flops | bytes accessed | tf_op | source)
XLA Modules:
  0.0 74.3 jit_solution(13368005371275311992)
XLA Ops:
  0.6 0.0 copy-start.6
  0.6 0.0 copy-start.1
  0.7 0.0 copy-start.4
  0.7 0.0 copy-start.5
  0.7 0.0 copy-start.3
  0.7 1.6 %bitcast_convert_fusion.embed = bf16[400,1024]{1,0:T(8,128)(2,1)S(1)} fusion(f32[1024,400]{0,1:T(8,128)} %param.8), kind=kLoop, calls=%fused_computation | loop fusion | flops 409600 | bytes 2457600 | tf_op jit(solution)/shard_map/convert_element_type | solution.py:205
  2.3 0.1 fusion
  2.3 4.0 %collective-permute-start = (bf16[400,512]{1,0:T(8,128)(2,1)S(1)}, bf16[400,512]{1,0:T(8,128)(2,1)S(1)}, u32[]{:S(2)}, u32[]{:S(2)}) collective-permute-start(bf16[400,512]{1,0:T(8,128)(2,1)S(1)} %get-tuple-element.46), channel_id=1, source_target_pairs={{0,64},{64,0},{128,192},{192,128},{256,320},{320,256},{384,448},{4... | collective-permute-start | bytes 1228808 | tf_op jit(solution)/shard_map/ppermute | solution.py:37
  6.4 1.9 %collective-permute-start.1 = (bf16[400,512]{1,0:T(8,128)(2,1)S(1)}, bf16[400,512]{1,0:T(8,128)(2,1)S(1)}, u32[]{:S(2)}, u32[]{:S(2)}) collective-permute-start(bf16[400,512]{1,0:T(8,128)(2,1)S(1)} %get-tuple-element.45), channel_id=1, source_target_pairs={{0,64},{64,0},{128,192},{192,128},{256,320},{320,256},{384,448},{4... | collective-permute-start | bytes 1228808 | tf_op jit(solution)/shard_map/ppermute | solution.py:37
  8.9 0.0 copy-done.6
  9.0 0.0 copy-done.1
  9.0 0.0 copy-done.4
  9.0 0.0 copy-done.5
  9.0 0.0 copy-done.3
  9.0 4.8 %shard_map.103 = (bf16[400,1024]{1,0:T(8,128)(2,1)S(1)}, f32[400,1024]{1,0:T(8,128)S(1)}, bf16[400,1024]{1,0:T(8,128)(2,1)S(1)}, bf16[1024,400]{1,0:T(8,128)(2,1...) custom-call(s32[8]{0:T(128)S(1)} %copy-done.6, s32[1]{0:T(128)S(6)} %copy.11.live, ...), custom_call_target="tpu_custom_call" | custom-call | flops 1677721600 | bytes 8388608 | tf_op jit(solution)/shard_map/pallas_call | solution.py:189
  13.8 0.0 collective-permute-done.other
  13.8 1.3 %shard_map.104 = (f32[1024,512]{1,0:T(8,128)S(1)}, f32[1024,1]{1,0:T(8,128)S(1)}, f32[1024,1]{1,0:T(8,128)S(1)}, f32[400,1024]{1,0:T(8,128)S(1)}) custom-call(bf16[400,512]{1,0:T(8,128)(2,1)S(1)} %collective-permute-done.other, bf16[1024,400]{1,0:T(8,128)(2,1)S(1)} %get-tuple-element.25.query_rows, f32[1024,1024]{1,0:T(8,128)S(1)} %get-tuple-element.26.bias, ...), custom_call_target="tpu_custom_call" | custom-call | flops 838860800 | bytes 8388608 | tf_op jit(solution)/shard_map/pallas_call | solution.py:189
  15.1 4.3 %collective-permute-done.1.rest = bf16[400,512]{1,0:T(8,128)(2,1)S(1)} collective-permute-done((bf16[400,512]{1,0:T(8,128)(2,1)S(1)}, bf16[400,512]{1,0:T(8,128)(2,1)S(1)}, u32[]{:S(2)}, u32[]{:S(2)}) %collective-permute-start.1) | collective-permute-done | bytes 409632 | tf_op jit(solution)/shard_map/ppermute | solution.py:37
  19.4 2.6 %shard_map.105 = (bf16[1024,1024]{1,0:T(8,128)(2,1)S(1)}, bf16[400,1024]{1,0:T(8,128)(2,1)S(1)}) custom-call(s32[1]{0:T(128)S(6)} %copy.11.live, bf16[400,512]{1,0:T(8,128)(2,1)S(1)} %collective-permute-done.1.rest, bf16[400,1024]{1,0:T(8,128)(2,1)S(1)} %get-tuple-element.24.query, bf16[1024,400]{1,0:T(8,128)(2,1)S(1)} %get-tuple-element.25.query_rows, ...), custom_call_target="tpu_custom_call" | custom-call | flops 1677721600 | bytes 8388608 | tf_op jit(solution)/shard_map/pallas_call | solution.py:189
  22.0 4.1 %collective-permute-start.2 = (bf16[400,1024]{1,0:T(8,128)(2,1)S(1)}, bf16[400,1024]{1,0:T(8,128)(2,1)S(1)}, u32[]{:S(2)}, u32[]{:S(2)}) collective-permute-start(bf16[400,1024]{1,0:T(8,128)(2,1)S(1)} %get-tuple-element.37), channel_id=1, source_target_pairs={{0,64},{64,0},{128,192},{192,128},{256,320},{320,256},{384,448},{4... | collective-permute-start | bytes 2457608 | tf_op jit(solution)/shard_map/ppermute | solution.py:37
  26.1 2.4 %shard_map.106 = (bf16[400,1024]{1,0:T(8,128)(2,1)S(1)}, bf16[64,8,128]{2,1,0:T(8,128)(2,1)S(1)}) custom-call(bf16[400,512]{1,0:T(8,128)(2,1)S(1)} %collective-permute-done.other, bf16[400,512]{1,0:T(8,128)(2,1)S(1)} %collective-permute-done.1.rest, bf16[1024,1024]{1,0:T(8,128)(2,1)S(1)} %get-tuple-element.32.softmax, ...), custom_call_target="tpu_custom_call" | custom-call | flops 1677721600 | bytes 8388608 | tf_op jit(solution)/shard_map/pallas_call | solution.py:189
  28.5 29.2 %all_to_all.10.terms = bf16[64,8,128]{2,1,0:T(8,128)(2,1)S(1)} all-to-all(bf16[64,8,128]{2,1,0:T(8,128)(2,1)S(1)} %get-tuple-element.38), channel_id=1, replica_groups=mesh['y'=8,'x_hi'=2,'x_lo'=2,'z'=8,'core'=2] {'x_hi','x_lo','z','core'}, dimensions={0} | all-to-all | bytes 262144 | tf_op jit(solution)/shard_map/all_to_all | solution.py:41
  57.7 0.7 shard_map.108
  58.4 0.0 copy-start
  58.4 0.0 collective-permute-done.2.received
  58.4 7.0 %all-to-all-start.1 = ((bf16[32,8,128]{2,1,0:T(8,128)(2,1)}), bf16[32,8,128]{2,1,0:T(8,128)(2,1)S(1)}, u32[]{:S(2)}, u32[]{:S(2)}) async-start(bf16[32,8,128]{2,1,0:T(8,128)(2,1)} %shard_map.108), calls=%async_computation.1 | async-start | bytes 131072 | tf_op jit(solution)/shard_map/all_to_all | solution.py:41
  65.4 1.0 %shard_map.107.source_grad = f32[400,1024]{1,0:T(8,128)S(1)} custom-call(bf16[400,1024]{1,0:T(8,128)(2,1)S(1)} %get-tuple-element.36.left_grad, s32[1,1024]{1,0:T(1,128)S(1)} %bitcast.14), custom_call_target="tpu_custom_call" | custom-call | flops 838860800 | bytes 8388608 | tf_op jit(solution)/shard_map/pallas_call | solution.py:189
  66.4 0.0 copy-done
  66.4 0.0 copy-done.2
  66.5 1.7 %shard_map.109 = (f32[400,1024]{1,0:T(8,128)}, f32[1,1024]{1,0:T(1,128)}) custom-call(f32[400,1024]{1,0:T(8,128)S(1)} %bitcast.8, f32[1,1024]{1,0:T(1,128)S(1)} %bitcast.11, f32[400,1024]{1,0:T(8,128)S(1)} %shard_map.107.source_grad, bf16[400,1024]{1,0:T(8,128)(2,1)S(1)} %collective-permute-done.2.received), custom_call_target="tpu_custom_call" | custom-call | flops 8388608 | bytes 8388608 | tf_op jit(solution)/shard_map/pallas_call | solution.py:189
  68.2 5.5 %all-to-all-done.1.terms = bf16[32,8,128]{2,1,0:T(8,128)(2,1)S(1)} async-done(((bf16[32,8,128]{2,1,0:T(8,128)(2,1)}), bf16[32,8,128]{2,1,0:T(8,128)(2,1)S(1)}, u32[]{:S(2)}, u32[]{:S(2)}) %all-to-all-start.1) | async-done | bytes 65568 | tf_op jit(solution)/shard_map/all_to_all | solution.py:41
  73.7 0.6 shard_map.110
  (1 shorter events, 0.0 us)
Async XLA Ops:
  0.6 8.3 %copy-start.6 = (s32[8]{0:T(128)S(1)}, s32[8]{0:T(128)}, u32[]{:S(2)}) copy-start(s32[8]{0:T(128)} %starts.1) | copy-start | bytes 100
  0.6 8.3 %copy-start.1 = (s32[1024]{0:T(1024)S(1)}, s32[1024]{0:T(1024)}, u32[]{:S(2)}) copy-start(s32[1024]{0:T(1024)} %param.13) | copy-start | bytes 12292
  0.7 8.3 %copy-start.4 = (s32[1024]{0:T(1024)S(1)}, s32[1024]{0:T(1024)}, u32[]{:S(2)}) copy-start(s32[1024]{0:T(1024)} %param.12) | copy-start | bytes 12292
  0.7 8.3 %copy-start.5 = (s32[1024]{0:T(1024)S(1)}, s32[1024]{0:T(1024)}, u32[]{:S(2)}) copy-start(s32[1024]{0:T(1024)} %param.11) | copy-start | bytes 12292
  0.7 8.3 %copy-start.3 = (f32[8,400]{1,0:T(8,128)S(1)}, f32[8,400]{1,0:T(8,128)}, u32[]{:S(2)}) copy-start(f32[8,400]{1,0:T(8,128)} %relation.1) | copy-start | bytes 38404
  2.3 11.5 %collective-permute-start = (bf16[400,512]{1,0:T(8,128)(2,1)S(1)}, bf16[400,512]{1,0:T(8,128)(2,1)S(1)}, u32[]{:S(2)}, u32[]{:S(2)}) collective-permute-start(bf16[400,512]{1,0:T(8,128)(2,1)S(1)} %get-tuple-element.46), channel_id=1, source_target_pairs={{0,64},{64,0},{128,192},{192,128},{256,320},{320,256},{384,448},{4... | collective-permute-start | bytes 1228808 | tf_op jit(solution)/shard_map/ppermute | solution.py:37
  6.4 13.0 %collective-permute-start.1 = (bf16[400,512]{1,0:T(8,128)(2,1)S(1)}, bf16[400,512]{1,0:T(8,128)(2,1)S(1)}, u32[]{:S(2)}, u32[]{:S(2)}) collective-permute-start(bf16[400,512]{1,0:T(8,128)(2,1)S(1)} %get-tuple-element.45), channel_id=1, source_target_pairs={{0,64},{64,0},{128,192},{192,128},{256,320},{320,256},{384,448},{4... | collective-permute-start | bytes 1228808 | tf_op jit(solution)/shard_map/ppermute | solution.py:37
  22.0 36.4 %collective-permute-start.2 = (bf16[400,1024]{1,0:T(8,128)(2,1)S(1)}, bf16[400,1024]{1,0:T(8,128)(2,1)S(1)}, u32[]{:S(2)}, u32[]{:S(2)}) collective-permute-start(bf16[400,1024]{1,0:T(8,128)(2,1)S(1)} %get-tuple-element.37), channel_id=1, source_target_pairs={{0,64},{64,0},{128,192},{192,128},{256,320},{320,256},{384,448},{4... | collective-permute-start | bytes 2457608 | tf_op jit(solution)/shard_map/ppermute | solution.py:37
  58.4 8.1 %copy-start = (f32[1024,400]{0,1:T(8,128)S(1)}, f32[1024,400]{0,1:T(8,128)}, u32[]{:S(2)}) copy-start(f32[1024,400]{0,1:T(8,128)} %param.8) | copy-start | bytes 4915204
  58.4 8.1 %copy-start.2 = (f32[1024]{0:T(1024)S(1)}, f32[1024]{0:T(1024)}, u32[]{:S(2)}) copy-start(f32[1024]{0:T(1024)} %param.9) | copy-start | bytes 12292
  58.4 15.3 %all-to-all-start.1 = ((bf16[32,8,128]{2,1,0:T(8,128)(2,1)}), bf16[32,8,128]{2,1,0:T(8,128)(2,1)S(1)}, u32[]{:S(2)}, u32[]{:S(2)}) async-start(bf16[32,8,128]{2,1,0:T(8,128)(2,1)} %shard_map.108), calls=%async_computation.1 | async-start | bytes 131072 | tf_op jit(solution)/shard_map/all_to_all | solution.py:41

commit v3 on v2

--- a/solution.py
+++ b/solution.py
@@ -18,7 +18,7 @@
 PIECE = 128
 TILE = 256
 WIDE = 512
-CUT = 512
+CUT = 768
 LOG_TWO = 0.6931471805599453
 NEVER = -1e30
 
@@ -60,8 +60,8 @@
     return (row == index).astype(jnp.float32)
 
 
-def prepare_kernel(starts, live, embed, relation, lhs, rhs, kinds, source, rel_rows, query, query_rows, bias, target, target_grad):
-    rows, edges = embed.shape[1], lhs.shape[1]
+def prepare_kernel(starts, live, embed, embed_rest, relation, lhs, rhs, kinds, source, rel_rows, query, query_rows, bias, target, target_grad):
+    cut, rows, edges = embed.shape[1], target.shape[1], lhs.shape[1]
     rel_rows[...] = lax.dot_general(
         relation[...],
         one_hot(kinds[...], relation.shape[0]),
@@ -71,7 +71,8 @@
     )
     for at in range(0, edges, TILE):
         here = slice(at, at + TILE)
-        source_here = dot(embed[...], one_hot(lhs[:, here], rows).astype(jnp.bfloat16), NN)
+        left_hot = one_hot(lhs[:, here], rows).astype(jnp.bfloat16)
+        source_here = dot(embed[...], left_hot[:cut, :], NN) + dot(embed_rest[...], left_hot[cut:, :], NN)
         query_here = source_here * rel_rows[:, here]
         source[:, here] = source_here.astype(jnp.bfloat16)
         query[:, here] = query_here.astype(jnp.bfloat16)
@@ -202,8 +203,11 @@
     edges = lhs_rows.shape[0]
     bf16, f32 = jnp.bfloat16, jnp.float32
     columns = slab.T
-    embed = columns.astype(bf16)
-    other, rest = swapped(embed[:, :CUT]), swapped(embed[:, CUT:])
+    embed = columns[:, :CUT].astype(bf16)
+    other = swapped(embed)
+    embed, later = lax.optimization_barrier((embed, columns[:, CUT:]))
+    embed_rest = later.astype(bf16)
+    rest = swapped(embed_rest)
     lhs, rhs, kinds = (x.reshape(1, edges) for x in (lhs_rows, rhs_rows, rel_ids))
     work = 2 * rows * edges * width
     source, rel_rows, query, query_rows, bias, target, target_grad = call(
@@ -218,7 +222,7 @@
             ((width, rows), f32),
         ],
         (neg_start, live_edges),
-        (embed, relation, lhs, rhs, kinds),
+        (embed, embed_rest, relation, lhs, rhs, kinds),
         2 * work,
     )
     power, top, total, positives = call(

time: 74.6 us -> 73.7 us (0.988)
  local copies, waits for them, and re-layouts: 0.09 us -> 2.43 us
  waiting for transfers between devices: 9.83 us -> 8.07 us
  other arithmetic: 1.58 us -> 0 us
    slice x1 -> x2, local copies, waits for them, and re-layouts: 0.06 us -> 2.41 us  [the longest x1 1.38 us: on_device(): embed = columns[:, :CUT].astype(bf16)]
    ppermute x3, waiting for transfers between devices: 4.3 us -> 2.55 us  [swapped(): return lax.ppermute(x, 'y', [(i, i ^ 1) for i in range(lax.axis_size('y'))])]
    convert_element_type x1 -> x0, other arithmetic: 1.58 us -> none  [on_device(): embed = columns.astype(bf16)]
  transfers between devices with their start and end apart: 4 -> 4, of which waited for: 2 -> 3; matrix products, arithmetic and copies ran while one was open for 0% -> 1% of each run, Pallas kernels for 16% -> 17%
where the time goes in v3:
time: 73.7 us; the launch traced here: 73.4 us
  blocking collectives  29.2 us (40%)
  starting transfers between devices  17.1 us (23%)
  Pallas kernels  15.2 us (21%)
  waiting for transfers between devices  8.07 us (11%)
  local copies, waits for them, and re-layouts  2.43 us (3%)
  between operations  1.44 us (2%)
    all_to_all x1, blocking collectives, exchanged(): return lax.all_to_all(terms, axes, 0, 0)  29.2 us
    pallas_call x8, Pallas kernels, call(): pl.pallas_call(kernel, out_shape=[jax.ShapeDtypeStruct(shape, dtype) for...  15.2 us
    ppermute x3, starting transfers between devices, swapped(): return lax.ppermute(x, 'y', [(i, i ^ 1) for i in range(lax.axis_size('y'))])  10.1 us
    all_to_all x1, starting transfers between devices, exchanged(): return lax.all_to_all(terms, axes, 0, 0)  6.99 us
    all_to_all x1, waiting for transfers between devices, exchanged(): return lax.all_to_all(terms, axes, 0, 0)  5.52 us
    ppermute x3, waiting for transfers between devices, swapped(): return lax.ppermute(x, 'y', [(i, i ^ 1) for i in range(lax.axis_size('y'))])  2.55 us
  transfers between devices with their start and end apart: 4, of which 3 were waited for; matrix products, arithmetic and copies ran while one was open for 1% of the time, Pallas kernels for 17%

profile of v3, /device:TPU:1, one launch (start us, length us, event | category | flops | bytes accessed | tf_op | source)
XLA Modules:
  0.0 73.4 jit_solution(16726431961005429730)
XLA Ops:
  0.6 0.0 copy-start.6
  0.6 0.0 copy-start.1
  0.7 0.0 copy-start.4
  0.7 0.0 copy-start.5
  0.7 0.0 copy-start.3
  0.7 1.4 %slice.12.embed = bf16[400,768]{1,0:T(8,128)(2,1)S(1)} slice(f32[400,1024]{1,0:T(8,128)} %bitcast.7), slice={[0:400], [0:768]} | slice | bytes 1228800 | tf_op jit(solution)/shard_map/slice | solution.py:206
  2.1 4.0 %collective-permute-start = (bf16[400,768]{1,0:T(8,128)(2,1)S(1)}, bf16[400,768]{1,0:T(8,128)(2,1)S(1)}, u32[]{:S(2)}, u32[]{:S(2)}) collective-permute-start(bf16[400,768]{1,0:T(8,128)(2,1)S(1)} %slice.12.embed), channel_id=1, source_target_pairs={{0,64},{64,0},{128,192},{192,128},{256,320},{320,256},{384,448},{4... | collective-permute-start | bytes 1843208 | tf_op jit(solution)/shard_map/ppermute | solution.py:37
  6.1 1.0 %slice.10.embed_rest = bf16[400,256]{1,0:T(8,128)(2,1)S(1)} slice(f32[400,1024]{1,0:T(8,128)} %bitcast.8), slice={[0:400], [768:1024]} | slice | bytes 409600 | tf_op jit(solution)/shard_map/slice | solution.py:208
  7.1 1.9 %collective-permute-start.1 = (bf16[400,256]{1,0:T(8,128)(2,1)S(1)}, bf16[400,256]{1,0:T(8,128)(2,1)S(1)}, u32[]{:S(2)}, u32[]{:S(2)}) collective-permute-start(bf16[400,256]{1,0:T(8,128)(2,1)S(1)} %slice.10.embed_rest), channel_id=1, source_target_pairs={{0,64},{64,0},{128,192},{192,128},{256,320},{320,256},{384,448},{4... | collective-permute-start | bytes 614408 | tf_op jit(solution)/shard_map/ppermute | solution.py:37
  9.7 0.0 copy-done.6
  9.7 0.0 copy-done.1
  9.7 0.0 copy-done.4
  9.7 0.0 copy-done.5
  9.8 0.0 copy-done.3
  9.8 4.8 %shard_map.103 = (bf16[400,1024]{1,0:T(8,128)(2,1)S(1)}, f32[400,1024]{1,0:T(8,128)S(1)}, bf16[400,1024]{1,0:T(8,128)(2,1)S(1)}, bf16[1024,400]{1,0:T(8,128)(2,1...) custom-call(s32[8]{0:T(128)S(1)} %copy-done.6, s32[1]{0:T(128)S(6)} %copy.11.live, ...), custom_call_target="tpu_custom_call" | custom-call | flops 1677721600 | bytes 8388608 | tf_op jit(solution)/shard_map/pallas_call | solution.py:190
  14.6 0.1 collective-permute-done.other
  14.7 2.0 %shard_map.104 = (f32[1024,768]{1,0:T(8,128)S(1)}, f32[1024,1]{1,0:T(8,128)S(1)}, f32[1024,1]{1,0:T(8,128)S(1)}, f32[400,1024]{1,0:T(8,128)S(1)}) custom-call(bf16[400,768]{1,0:T(8,128)(2,1)S(1)} %collective-permute-done.other, bf16[1024,400]{1,0:T(8,128)(2,1)S(1)} %get-tuple-element.29.query_rows, f32[1024,1024]{1,0:T(8,128)S(1)} %get-tuple-element.30.bias, ...), custom_call_target="tpu_custom_call" | custom-call | flops 838860800 | bytes 8388608 | tf_op jit(solution)/shard_map/pallas_call | solution.py:190
  16.7 2.4 %collective-permute-done.1.rest = bf16[400,256]{1,0:T(8,128)(2,1)S(1)} collective-permute-done((bf16[400,256]{1,0:T(8,128)(2,1)S(1)}, bf16[400,256]{1,0:T(8,128)(2,1)S(1)}, u32[]{:S(2)}, u32[]{:S(2)}) %collective-permute-start.1) | collective-permute-done | bytes 204832 | tf_op jit(solution)/shard_map/ppermute | solution.py:37
  19.1 2.0 %shard_map.105 = (bf16[1024,1024]{1,0:T(8,128)(2,1)S(1)}, bf16[400,1024]{1,0:T(8,128)(2,1)S(1)}) custom-call(s32[1]{0:T(128)S(6)} %copy.11.live, bf16[400,256]{1,0:T(8,128)(2,1)S(1)} %collective-permute-done.1.rest, bf16[400,1024]{1,0:T(8,128)(2,1)S(1)} %get-tuple-element.28.query, bf16[1024,400]{1,0:T(8,128)(2,1)S(1)} %get-tuple-element.29.query_rows, ...), custom_call_target="tpu_custom_call" | custom-call | flops 1677721600 | bytes 8388608 | tf_op jit(solution)/shard_map/pallas_call | solution.py:190
  21.2 4.1 %collective-permute-start.2 = (bf16[400,1024]{1,0:T(8,128)(2,1)S(1)}, bf16[400,1024]{1,0:T(8,128)(2,1)S(1)}, u32[]{:S(2)}, u32[]{:S(2)}) collective-permute-start(bf16[400,1024]{1,0:T(8,128)(2,1)S(1)} %get-tuple-element.41), channel_id=1, source_target_pairs={{0,64},{64,0},{128,192},{192,128},{256,320},{320,256},{384,448},{4... | collective-permute-start | bytes 2457608 | tf_op jit(solution)/shard_map/ppermute | solution.py:37
  25.3 2.2 %shard_map.106 = (bf16[400,1024]{1,0:T(8,128)(2,1)S(1)}, bf16[64,8,128]{2,1,0:T(8,128)(2,1)S(1)}) custom-call(bf16[400,768]{1,0:T(8,128)(2,1)S(1)} %collective-permute-done.other, bf16[400,256]{1,0:T(8,128)(2,1)S(1)} %collective-permute-done.1.rest, bf16[1024,1024]{1,0:T(8,128)(2,1)S(1)} %get-tuple-element.36.softmax, ...), custom_call_target="tpu_custom_call" | custom-call | flops 1677721600 | bytes 8388608 | tf_op jit(solution)/shard_map/pallas_call | solution.py:190
  27.5 29.2 %all_to_all.10.terms = bf16[64,8,128]{2,1,0:T(8,128)(2,1)S(1)} all-to-all(bf16[64,8,128]{2,1,0:T(8,128)(2,1)S(1)} %get-tuple-element.42), channel_id=1, replica_groups=mesh['y'=8,'x_hi'=2,'x_lo'=2,'z'=8,'core'=2] {'x_hi','x_lo','z','core'}, dimensions={0} | all-to-all | bytes 262144 | tf_op jit(solution)/shard_map/all_to_all | solution.py:41
  56.7 0.7 shard_map.108
  57.4 0.0 copy-start
  57.4 0.0 collective-permute-done.2.received
  57.4 7.0 %all-to-all-start.1 = ((bf16[32,8,128]{2,1,0:T(8,128)(2,1)}), bf16[32,8,128]{2,1,0:T(8,128)(2,1)S(1)}, u32[]{:S(2)}, u32[]{:S(2)}) async-start(bf16[32,8,128]{2,1,0:T(8,128)(2,1)} %shard_map.108), calls=%async_computation.1 | async-start | bytes 131072 | tf_op jit(solution)/shard_map/all_to_all | solution.py:41
  64.4 1.1 %shard_map.107.source_grad = f32[400,1024]{1,0:T(8,128)S(1)} custom-call(bf16[400,1024]{1,0:T(8,128)(2,1)S(1)} %get-tuple-element.40.left_grad, s32[1,1024]{1,0:T(1,128)S(1)} %bitcast.15), custom_call_target="tpu_custom_call" | custom-call | flops 838860800 | bytes 8388608 | tf_op jit(solution)/shard_map/pallas_call | solution.py:190
  65.5 0.0 copy-done
  65.5 0.0 copy-done.2
  65.5 1.7 %shard_map.109 = (f32[400,1024]{1,0:T(8,128)}, f32[1,1024]{1,0:T(1,128)}) custom-call(f32[400,1024]{1,0:T(8,128)S(1)} %bitcast.9, f32[1,1024]{1,0:T(1,128)S(1)} %bitcast.12, f32[400,1024]{1,0:T(8,128)S(1)} %shard_map.107.source_grad, bf16[400,1024]{1,0:T(8,128)(2,1)S(1)} %collective-permute-done.2.received), custom_call_target="tpu_custom_call" | custom-call | flops 8388608 | bytes 8388608 | tf_op jit(solution)/shard_map/pallas_call | solution.py:190
  67.2 5.5 %all-to-all-done.1.terms = bf16[32,8,128]{2,1,0:T(8,128)(2,1)S(1)} async-done(((bf16[32,8,128]{2,1,0:T(8,128)(2,1)}), bf16[32,8,128]{2,1,0:T(8,128)(2,1)S(1)}, u32[]{:S(2)}, u32[]{:S(2)}) %all-to-all-start.1) | async-done | bytes 65568 | tf_op jit(solution)/shard_map/all_to_all | solution.py:41
  72.7 0.6 shard_map.110
  (1 shorter events, 0.0 us)
Async XLA Ops:
  0.6 9.1 %copy-start.6 = (s32[8]{0:T(128)S(1)}, s32[8]{0:T(128)}, u32[]{:S(2)}) copy-start(s32[8]{0:T(128)} %starts.1) | copy-start | bytes 100
  0.6 9.1 %copy-start.1 = (s32[1024]{0:T(1024)S(1)}, s32[1024]{0:T(1024)}, u32[]{:S(2)}) copy-start(s32[1024]{0:T(1024)} %param.13) | copy-start | bytes 12292
  0.7 9.1 %copy-start.4 = (s32[1024]{0:T(1024)S(1)}, s32[1024]{0:T(1024)}, u32[]{:S(2)}) copy-start(s32[1024]{0:T(1024)} %param.12) | copy-start | bytes 12292
  0.7 9.1 %copy-start.5 = (s32[1024]{0:T(1024)S(1)}, s32[1024]{0:T(1024)}, u32[]{:S(2)}) copy-start(s32[1024]{0:T(1024)} %param.11) | copy-start | bytes 12292
  0.7 9.1 %copy-start.3 = (f32[8,400]{1,0:T(8,128)S(1)}, f32[8,400]{1,0:T(8,128)}, u32[]{:S(2)}) copy-start(f32[8,400]{1,0:T(8,128)} %relation.1) | copy-start | bytes 38404
  2.1 12.7 %collective-permute-start = (bf16[400,768]{1,0:T(8,128)(2,1)S(1)}, bf16[400,768]{1,0:T(8,128)(2,1)S(1)}, u32[]{:S(2)}, u32[]{:S(2)}) collective-permute-start(bf16[400,768]{1,0:T(8,128)(2,1)S(1)} %slice.12.embed), channel_id=1, source_target_pairs={{0,64},{64,0},{128,192},{192,128},{256,320},{320,256},{384,448},{4... | collective-permute-start | bytes 1843208 | tf_op jit(solution)/shard_map/ppermute | solution.py:37
  7.1 12.0 %collective-permute-start.1 = (bf16[400,256]{1,0:T(8,128)(2,1)S(1)}, bf16[400,256]{1,0:T(8,128)(2,1)S(1)}, u32[]{:S(2)}, u32[]{:S(2)}) collective-permute-start(bf16[400,256]{1,0:T(8,128)(2,1)S(1)} %slice.10.embed_rest), channel_id=1, source_target_pairs={{0,64},{64,0},{128,192},{192,128},{256,320},{320,256},{384,448},{4... | collective-permute-start | bytes 614408 | tf_op jit(solution)/shard_map/ppermute | solution.py:37
  21.2 36.2 %collective-permute-start.2 = (bf16[400,1024]{1,0:T(8,128)(2,1)S(1)}, bf16[400,1024]{1,0:T(8,128)(2,1)S(1)}, u32[]{:S(2)}, u32[]{:S(2)}) collective-permute-start(bf16[400,1024]{1,0:T(8,128)(2,1)S(1)} %get-tuple-element.41), channel_id=1, source_target_pairs={{0,64},{64,0},{128,192},{192,128},{256,320},{320,256},{384,448},{4... | collective-permute-start | bytes 2457608 | tf_op jit(solution)/shard_map/ppermute | solution.py:37
  57.4 8.1 %copy-start = (f32[1024,400]{0,1:T(8,128)S(1)}, f32[1024,400]{0,1:T(8,128)}, u32[]{:S(2)}) copy-start(f32[1024,400]{0,1:T(8,128)} %param.8) | copy-start | bytes 4915204
  57.4 8.1 %copy-start.2 = (f32[1024]{0:T(1024)S(1)}, f32[1024]{0:T(1024)}, u32[]{:S(2)}) copy-start(f32[1024]{0:T(1024)} %param.9) | copy-start | bytes 12292
  57.4 15.3 %all-to-all-start.1 = ((bf16[32,8,128]{2,1,0:T(8,128)(2,1)}), bf16[32,8,128]{2,1,0:T(8,128)(2,1)S(1)}, u32[]{:S(2)}, u32[]{:S(2)}) async-start(bf16[32,8,128]{2,1,0:T(8,128)(2,1)} %shard_map.108), calls=%async_computation.1 | async-start | bytes 131072 | tf_op jit(solution)/shard_map/all_to_all | solution.py:41

commit v4 on v3

--- a/solution.py
+++ b/solution.py
@@ -17,7 +17,7 @@
 FAR = ("y", "x_lo", "core")
 PIECE = 128
 TILE = 256
-WIDE = 512
+WIDE = 1024
 CUT = 768
 LOG_TWO = 0.6931471805599453
 NEVER = -1e30
@@ -48,11 +48,6 @@
 
 def dot(a, b, dims):
     return lax.dot_general(a, b, dims, preferred_element_type=jnp.float32)
-
-
-def split(x):
-    high = x.astype(jnp.bfloat16)
-    return high, (x - high.astype(jnp.float32)).astype(jnp.bfloat16)
 
 
 def one_hot(index, classes):
@@ -93,7 +88,7 @@
     target_grad[...] = -dot(query[...], target[...], NN)
 
 
-def first_kernel(other, query_rows, bias, target, power, top, total, positives):
+def first_kernel(other, query_rows, bias, target, power, top, total, positives, negatives):
     edges, cut = bias.shape[0], other.shape[1]
     for at in range(0, edges, TILE):
         here = slice(at, at + TILE)
@@ -104,10 +99,11 @@
         top[here, :] = top_here
         total[here, :] = jnp.sum(power_here, axis=1, keepdims=True)
         positives[:, here] = dot(other[...], target[here, :cut], NT)
+        negatives[:, here] = dot(other[...], power_here.astype(jnp.bfloat16), NT)
 
 
 def second_kernel(
-    live, rest, query, query_rows, bias, target_grad, power, top, total, softmax, sent_grad
+    live, rest, query, query_rows, bias, target_grad, power, top, total, softmax, sent_grad, scales
 ):
     edges, cut = power.shape
     for at in range(0, edges, TILE):
@@ -119,27 +115,29 @@
         total_here = jnp.sum(power_here, axis=1, keepdims=True) + total[here, :] * scale
         slot = lax.broadcasted_iota(jnp.int32, total_here.shape, 0) + at
         weight = jnp.where(slot < live[0], 1.0, 0.0) / total_here
-        softmax[here, :cut] = (power[here, :] * (scale * weight)).astype(jnp.bfloat16)
+        scale = scale * weight
+        scales[:, here] = jnp.broadcast_to(scale, (TILE, BLOCK)).T[:1, :]
+        softmax[here, :cut] = (power[here, :] * scale).astype(jnp.bfloat16)
         softmax[here, cut:] = (power_here * weight).astype(jnp.bfloat16)
     sent_grad[...] = (target_grad[...] + dot(query[...], softmax[...], NN)).astype(jnp.bfloat16)
 
 
 def relation_kernel(
-    near_pieces, other, rest, softmax, target, positives, source, rel_rows, kinds, left_grad, terms
+    near_pieces, rest, softmax, target, positives, negatives, scales, source, rel_rows, kinds, left_grad, terms
 ):
-    edges, cut = softmax.shape[0], other.shape[1]
+    edges, cut = softmax.shape[0], softmax.shape[1] - rest.shape[1]
     part = jnp.zeros((source.shape[0], terms.shape[1]), jnp.float32)
     for at in range(0, edges, WIDE):
         here = slice(at, at + WIDE)
         dquery = (
-            dot(other[...], softmax[here, :cut], NT)
+            negatives[:, here] * scales[:, here]
+            - positives[:, here]
             + dot(rest[...], softmax[here, cut:], NT)
             - dot(rest[...], target[here, cut:], NT)
-            - positives[:, here]
         )
         kind_hot = one_hot(kinds[:, here], part.shape[1]).astype(jnp.bfloat16)
-        high, low = split(dquery * source[:, here].astype(jnp.float32))
-        part = part + (dot(high, kind_hot, NT) + dot(low, kind_hot, NT))
+        change = (dquery * source[:, here].astype(jnp.float32)).astype(jnp.bfloat16)
+        part = part + dot(change, kind_hot, NT)
         left_grad[:, here] = (dquery * rel_rows[:, here]).astype(jnp.bfloat16)
     part = part.T
     part = jnp.concatenate([part, jnp.zeros((part.shape[0], -part.shape[1] % PIECE), part.dtype)], axis=1)
@@ -225,16 +223,16 @@
         (embed, embed_rest, relation, lhs, rhs, kinds),
         2 * work,
     )
-    power, top, total, positives = call(
+    power, top, total, positives, negatives = call(
         first_kernel,
-        [((edges, CUT), f32), ((edges, 1), f32), ((edges, 1), f32), ((width, edges), f32)],
+        [((edges, CUT), f32), ((edges, 1), f32), ((edges, 1), f32)] + [((width, edges), f32)] * 2,
         (),
         (other, query_rows, bias, target),
         work,
     )
-    softmax, sent_grad = call(
+    softmax, sent_grad, scales = call(
         second_kernel,
-        [((edges, rows), bf16), ((width, rows), bf16)],
+        [((edges, rows), bf16), ((width, rows), bf16), ((1, edges), f32)],
         (live_edges,),
         (rest, query, query_rows, bias, target_grad, power, top, total),
         2 * work,
@@ -246,7 +244,7 @@
         functools.partial(relation_kernel, near),
         [((width, edges), bf16), ((len(near),) + piece, bf16)],
         (),
-        (other, rest, softmax, target, positives, source, rel_rows, kinds),
+        (rest, softmax, target, positives, negatives, scales, source, rel_rows, kinds),
         2 * work,
     )
     terms = exchanged(terms, NEAR)

time: 73.7 us -> 72.9 us (0.989)
  waiting for transfers between devices: 8.07 us -> 6.77 us
    ppermute x3, waiting for transfers between devices: 2.55 us -> 1.24 us  [swapped(): return lax.ppermute(x, 'y', [(i, i ^ 1) for i in range(lax.axis_size('y'))])]
  transfers between devices with their start and end apart: 4 -> 4, of which waited for: 3 -> 3; matrix products, arithmetic and copies ran while one was open for 1% -> 1% of each run, Pallas kernels for 17% -> 18%
where the time goes in v4:
time: 72.9 us; the launch traced here: 72.5 us
  blocking collectives  29.3 us (40%)
  starting transfers between devices  17.1 us (23%)
  Pallas kernels  15.6 us (21%)
  waiting for transfers between devices  6.77 us (9%)
  local copies, waits for them, and re-layouts  2.43 us (3%)
  between operations  1.45 us (2%)
    all_to_all x1, blocking collectives, exchanged(): return lax.all_to_all(terms, axes, 0, 0)  29.3 us
    pallas_call x8, Pallas kernels, call(): pl.pallas_call(kernel, out_shape=[jax.ShapeDtypeStruct(shape, dtype) for...  15.6 us
    ppermute x3, starting transfers between devices, swapped(): return lax.ppermute(x, 'y', [(i, i ^ 1) for i in range(lax.axis_size('y'))])  10.1 us
    all_to_all x1, starting transfers between devices, exchanged(): return lax.all_to_all(terms, axes, 0, 0)  6.99 us
    all_to_all x1, waiting for transfers between devices, exchanged(): return lax.all_to_all(terms, axes, 0, 0)  5.52 us
  transfers between devices with their start and end apart: 4, of which 3 were waited for; matrix products, arithmetic and copies ran while one was open for 1% of the time, Pallas kernels for 18%

profile of v4, /device:TPU:1, one launch (start us, length us, event | category | flops | bytes accessed | tf_op | source)
XLA Modules:
  0.0 72.5 jit_solution(5219520907999671416)
XLA Ops:
  0.6 0.0 copy-start.6
  0.6 0.0 copy-start.1
  0.7 0.0 copy-start.4
  0.7 0.0 copy-start.5
  0.7 0.0 copy-start.3
  0.7 1.4 %slice.12.embed = bf16[400,768]{1,0:T(8,128)(2,1)S(1)} slice(f32[400,1024]{1,0:T(8,128)} %bitcast.7), slice={[0:400], [0:768]} | slice | bytes 1228800 | tf_op jit(solution)/shard_map/slice | solution.py:204
  2.1 4.0 %collective-permute-start.1 = (bf16[400,768]{1,0:T(8,128)(2,1)S(1)}, bf16[400,768]{1,0:T(8,128)(2,1)S(1)}, u32[]{:S(2)}, u32[]{:S(2)}) collective-permute-start(bf16[400,768]{1,0:T(8,128)(2,1)S(1)} %slice.12.embed), channel_id=1, source_target_pairs={{0,64},{64,0},{128,192},{192,128},{256,320},{320,256},{384,448},{4... | collective-permute-start | bytes 1843208 | tf_op jit(solution)/shard_map/ppermute | solution.py:37
  6.1 1.0 %slice.10.embed_rest = bf16[400,256]{1,0:T(8,128)(2,1)S(1)} slice(f32[400,1024]{1,0:T(8,128)} %bitcast.8), slice={[0:400], [768:1024]} | slice | bytes 409600 | tf_op jit(solution)/shard_map/slice | solution.py:206
  7.1 1.9 %collective-permute-start = (bf16[400,256]{1,0:T(8,128)(2,1)S(1)}, bf16[400,256]{1,0:T(8,128)(2,1)S(1)}, u32[]{:S(2)}, u32[]{:S(2)}) collective-permute-start(bf16[400,256]{1,0:T(8,128)(2,1)S(1)} %slice.10.embed_rest), channel_id=1, source_target_pairs={{0,64},{64,0},{128,192},{192,128},{256,320},{320,256},{384,448},{4... | collective-permute-start | bytes 614408 | tf_op jit(solution)/shard_map/ppermute | solution.py:37
  9.7 0.0 copy-done.6
  9.7 0.0 copy-done.1
  9.7 0.0 copy-done.4
  9.7 0.0 copy-done.5
  9.8 0.0 copy-done.3
  9.8 4.8 %shard_map.103 = (bf16[400,1024]{1,0:T(8,128)(2,1)S(1)}, f32[400,1024]{1,0:T(8,128)S(1)}, bf16[400,1024]{1,0:T(8,128)(2,1)S(1)}, bf16[1024,400]{1,0:T(8,128)(2,1...) custom-call(s32[8]{0:T(128)S(1)} %copy-done.6, s32[1]{0:T(128)S(6)} %copy.11.live, ...), custom_call_target="tpu_custom_call" | custom-call | flops 1677721600 | bytes 8388608 | tf_op jit(solution)/shard_map/pallas_call | solution.py:188
  14.6 0.1 collective-permute-done.1.other
  14.7 3.3 %shard_map.104 = (f32[1024,768]{1,0:T(8,128)S(1)}, f32[1024,1]{1,0:T(8,128)S(1)}, f32[1024,1]{1,0:T(8,128)S(1)}, f32[400,1024]{1,0:T(8,128)S(1)}, f32[400,1024]{1,0:T(8,128)S(1)}) custom-call(bf16[400,768]{1,0:T(8,128)(2,1)S(1)} %collective-permute-done.1.other, bf16[1024,400]{1,0:T(8,128)(2,1)S(1)} %get-tuple-element.31.query_rows, ...), custom_call_target="tpu_custom_call" | custom-call | flops 838860800 | bytes 8388608 | tf_op jit(solution)/shard_map/pallas_call | solution.py:188
  18.0 1.1 %collective-permute-done.rest = bf16[400,256]{1,0:T(8,128)(2,1)S(1)} collective-permute-done((bf16[400,256]{1,0:T(8,128)(2,1)S(1)}, bf16[400,256]{1,0:T(8,128)(2,1)S(1)}, u32[]{:S(2)}, u32[]{:S(2)}) %collective-permute-start) | collective-permute-done | bytes 204832 | tf_op jit(solution)/shard_map/ppermute | solution.py:37
  19.1 2.0 %shard_map.105 = (bf16[1024,1024]{1,0:T(8,128)(2,1)S(1)}, bf16[400,1024]{1,0:T(8,128)(2,1)S(1)}, f32[1,1024]{1,0:T(1,128)S(1)}) custom-call(s32[1]{0:T(128)S(6)} %copy.11.live, bf16[400,256]{1,0:T(8,128)(2,1)S(1)} %collective-permute-done.rest, bf16[400,1024]{1,0:T(8,128)(2,1)S(1)} %get-tuple-element.30.query, ...), custom_call_target="tpu_custom_call" | custom-call | flops 1677721600 | bytes 8388608 | tf_op jit(solution)/shard_map/pallas_call | solution.py:188
  21.2 4.1 %collective-permute-start.2 = (bf16[400,1024]{1,0:T(8,128)(2,1)S(1)}, bf16[400,1024]{1,0:T(8,128)(2,1)S(1)}, u32[]{:S(2)}, u32[]{:S(2)}) collective-permute-start(bf16[400,1024]{1,0:T(8,128)(2,1)S(1)} %get-tuple-element.45), channel_id=1, source_target_pairs={{0,64},{64,0},{128,192},{192,128},{256,320},{320,256},{384,448},{4... | collective-permute-start | bytes 2457608 | tf_op jit(solution)/shard_map/ppermute | solution.py:37
  25.3 1.3 %shard_map.106 = (bf16[400,1024]{1,0:T(8,128)(2,1)S(1)}, bf16[64,8,128]{2,1,0:T(8,128)(2,1)S(1)}) custom-call(bf16[400,256]{1,0:T(8,128)(2,1)S(1)} %collective-permute-done.rest, bf16[1024,1024]{1,0:T(8,128)(2,1)S(1)} %get-tuple-element.38.softmax, bf16[1024,1024]{1,0:T(8,128)(2,1)S(1)} %get-tuple-element.34.target, ...), custom_call_target="tpu_custom_call" | custom-call | flops 1677721600 | bytes 8388608 | tf_op jit(solution)/shard_map/pallas_call | solution.py:188
  26.6 29.3 %all_to_all.10.terms = bf16[64,8,128]{2,1,0:T(8,128)(2,1)S(1)} all-to-all(bf16[64,8,128]{2,1,0:T(8,128)(2,1)S(1)} %get-tuple-element.46), channel_id=1, replica_groups=mesh['y'=8,'x_hi'=2,'x_lo'=2,'z'=8,'core'=2] {'x_hi','x_lo','z','core'}, dimensions={0} | all-to-all | bytes 262144 | tf_op jit(solution)/shard_map/all_to_all | solution.py:41
  55.9 0.7 shard_map.108
  56.6 0.0 copy-start
  56.6 0.0 collective-permute-done.2.received
  56.6 7.0 %all-to-all-start.1 = ((bf16[32,8,128]{2,1,0:T(8,128)(2,1)}), bf16[32,8,128]{2,1,0:T(8,128)(2,1)S(1)}, u32[]{:S(2)}, u32[]{:S(2)}) async-start(bf16[32,8,128]{2,1,0:T(8,128)(2,1)} %shard_map.108), calls=%async_computation.1 | async-start | bytes 131072 | tf_op jit(solution)/shard_map/all_to_all | solution.py:41
  63.6 1.1 %shard_map.107.source_grad = f32[400,1024]{1,0:T(8,128)S(1)} custom-call(bf16[400,1024]{1,0:T(8,128)(2,1)S(1)} %get-tuple-element.44.left_grad, s32[1,1024]{1,0:T(1,128)S(1)} %bitcast.15), custom_call_target="tpu_custom_call" | custom-call | flops 838860800 | bytes 8388608 | tf_op jit(solution)/shard_map/pallas_call | solution.py:188
  64.6 0.0 copy-done
  64.6 0.0 copy-done.2
  64.7 1.7 %shard_map.109 = (f32[400,1024]{1,0:T(8,128)}, f32[1,1024]{1,0:T(1,128)}) custom-call(f32[400,1024]{1,0:T(8,128)S(1)} %bitcast.9, f32[1,1024]{1,0:T(1,128)S(1)} %bitcast.12, f32[400,1024]{1,0:T(8,128)S(1)} %shard_map.107.source_grad, bf16[400,1024]{1,0:T(8,128)(2,1)S(1)} %collective-permute-done.2.received), custom_call_target="tpu_custom_call" | custom-call | flops 8388608 | bytes 8388608 | tf_op jit(solution)/shard_map/pallas_call | solution.py:188
  66.4 5.5 %all-to-all-done.1.terms = bf16[32,8,128]{2,1,0:T(8,128)(2,1)S(1)} async-done(((bf16[32,8,128]{2,1,0:T(8,128)(2,1)}), bf16[32,8,128]{2,1,0:T(8,128)(2,1)S(1)}, u32[]{:S(2)}, u32[]{:S(2)}) %all-to-all-start.1) | async-done | bytes 65568 | tf_op jit(solution)/shard_map/all_to_all | solution.py:41
  71.9 0.6 shard_map.110
  (1 shorter events, 0.0 us)
Async XLA Ops:
  0.6 9.1 %copy-start.6 = (s32[8]{0:T(128)S(1)}, s32[8]{0:T(128)}, u32[]{:S(2)}) copy-start(s32[8]{0:T(128)} %starts.1) | copy-start | bytes 100
  0.6 9.1 %copy-start.1 = (s32[1024]{0:T(1024)S(1)}, s32[1024]{0:T(1024)}, u32[]{:S(2)}) copy-start(s32[1024]{0:T(1024)} %param.13) | copy-start | bytes 12292
  0.7 9.1 %copy-start.4 = (s32[1024]{0:T(1024)S(1)}, s32[1024]{0:T(1024)}, u32[]{:S(2)}) copy-start(s32[1024]{0:T(1024)} %param.12) | copy-start | bytes 12292
  0.7 9.1 %copy-start.5 = (s32[1024]{0:T(1024)S(1)}, s32[1024]{0:T(1024)}, u32[]{:S(2)}) copy-start(s32[1024]{0:T(1024)} %param.11) | copy-start | bytes 12292
  0.7 9.1 %copy-start.3 = (f32[8,400]{1,0:T(8,128)S(1)}, f32[8,400]{1,0:T(8,128)}, u32[]{:S(2)}) copy-start(f32[8,400]{1,0:T(8,128)} %relation.1) | copy-start | bytes 38404
  2.1 12.7 %collective-permute-start.1 = (bf16[400,768]{1,0:T(8,128)(2,1)S(1)}, bf16[400,768]{1,0:T(8,128)(2,1)S(1)}, u32[]{:S(2)}, u32[]{:S(2)}) collective-permute-start(bf16[400,768]{1,0:T(8,128)(2,1)S(1)} %slice.12.embed), channel_id=1, source_target_pairs={{0,64},{64,0},{128,192},{192,128},{256,320},{320,256},{384,448},{4... | collective-permute-start | bytes 1843208 | tf_op jit(solution)/shard_map/ppermute | solution.py:37
  7.1 12.0 %collective-permute-start = (bf16[400,256]{1,0:T(8,128)(2,1)S(1)}, bf16[400,256]{1,0:T(8,128)(2,1)S(1)}, u32[]{:S(2)}, u32[]{:S(2)}) collective-permute-start(bf16[400,256]{1,0:T(8,128)(2,1)S(1)} %slice.10.embed_rest), channel_id=1, source_target_pairs={{0,64},{64,0},{128,192},{192,128},{256,320},{320,256},{384,448},{4... | collective-permute-start | bytes 614408 | tf_op jit(solution)/shard_map/ppermute | solution.py:37
  21.2 35.4 %collective-permute-start.2 = (bf16[400,1024]{1,0:T(8,128)(2,1)S(1)}, bf16[400,1024]{1,0:T(8,128)(2,1)S(1)}, u32[]{:S(2)}, u32[]{:S(2)}) collective-permute-start(bf16[400,1024]{1,0:T(8,128)(2,1)S(1)} %get-tuple-element.45), channel_id=1, source_target_pairs={{0,64},{64,0},{128,192},{192,128},{256,320},{320,256},{384,448},{4... | collective-permute-start | bytes 2457608 | tf_op jit(solution)/shard_map/ppermute | solution.py:37
  56.6 8.1 %copy-start = (f32[1024,400]{0,1:T(8,128)S(1)}, f32[1024,400]{0,1:T(8,128)}, u32[]{:S(2)}) copy-start(f32[1024,400]{0,1:T(8,128)} %param.8) | copy-start | bytes 4915204
  56.6 8.1 %copy-start.2 = (f32[1024]{0:T(1024)S(1)}, f32[1024]{0:T(1024)}, u32[]{:S(2)}) copy-start(f32[1024]{0:T(1024)} %param.9) | copy-start | bytes 12292
  56.6 15.3 %all-to-all-start.1 = ((bf16[32,8,128]{2,1,0:T(8,128)(2,1)}), bf16[32,8,128]{2,1,0:T(8,128)(2,1)S(1)}, u32[]{:S(2)}, u32[]{:S(2)}) async-start(bf16[32,8,128]{2,1,0:T(8,128)(2,1)} %shard_map.108), calls=%async_computation.1 | async-start | bytes 131072 | tf_op jit(solution)/shard_map/all_to_all | solution.py:41

commit v5 on v4

--- a/solution.py
+++ b/solution.py
@@ -17,6 +17,7 @@
 FAR = ("y", "x_lo", "core")
 PIECE = 128
 TILE = 256
+HALF = 512
 WIDE = 1024
 CUT = 768
 LOG_TWO = 0.6931471805599453
@@ -90,8 +91,8 @@
 
 def first_kernel(other, query_rows, bias, target, power, top, total, positives, negatives):
     edges, cut = bias.shape[0], other.shape[1]
-    for at in range(0, edges, TILE):
-        here = slice(at, at + TILE)
+    for at in range(0, edges, HALF):
+        here = slice(at, at + HALF)
         score = dot(query_rows[here, :], other[...], NN) + bias[here, :cut]
         top_here = jnp.max(score, axis=1, keepdims=True)
         power_here = jnp.exp(score - top_here)

time: 72.9 us -> 72.8 us (level)
  transfers between devices with their start and end apart: 4 -> 4, of which waited for: 3 -> 3; matrix products, arithmetic and copies ran while one was open for 1% -> 1% of each run, Pallas kernels for 18% -> 17%
where the time goes in v5:
time: 72.8 us; the launch traced here: 72.5 us
  blocking collectives  29.2 us (40%)
  starting transfers between devices  17.1 us (23%)
  Pallas kernels  15.2 us (21%)
  waiting for transfers between devices  7.14 us (10%)
  local copies, waits for them, and re-layouts  2.43 us (3%)
  between operations  1.44 us (2%)
    all_to_all x1, blocking collectives, exchanged(): return lax.all_to_all(terms, axes, 0, 0)  29.2 us
    pallas_call x8, Pallas kernels, call(): pl.pallas_call(kernel, out_shape=[jax.ShapeDtypeStruct(shape, dtype) for...  15.2 us
    ppermute x3, starting transfers between devices, swapped(): return lax.ppermute(x, 'y', [(i, i ^ 1) for i in range(lax.axis_size('y'))])  10.1 us
    all_to_all x1, starting transfers between devices, exchanged(): return lax.all_to_all(terms, axes, 0, 0)  6.99 us
    all_to_all x1, waiting for transfers between devices, exchanged(): return lax.all_to_all(terms, axes, 0, 0)  5.52 us
    ppermute x3, waiting for transfers between devices, swapped(): return lax.ppermute(x, 'y', [(i, i ^ 1) for i in range(lax.axis_size('y'))])  1.62 us
  transfers between devices with their start and end apart: 4, of which 3 were waited for; matrix products, arithmetic and copies ran while one was open for 1% of the time, Pallas kernels for 17%

profile of v5, /device:TPU:1, one launch (start us, length us, event | category | flops | bytes accessed | tf_op | source)
XLA Modules:
  0.0 72.5 jit_solution(7242638763244058905)
XLA Ops:
  0.6 0.0 copy-start.6
  0.6 0.0 copy-start.1
  0.7 0.0 copy-start.4
  0.7 0.0 copy-start.5
  0.7 0.0 copy-start.3
  0.7 1.4 %slice.12.embed = bf16[400,768]{1,0:T(8,128)(2,1)S(1)} slice(f32[400,1024]{1,0:T(8,128)} %bitcast.7), slice={[0:400], [0:768]} | slice | bytes 1228800 | tf_op jit(solution)/shard_map/slice | solution.py:205
  2.1 4.0 %collective-permute-start.1 = (bf16[400,768]{1,0:T(8,128)(2,1)S(1)}, bf16[400,768]{1,0:T(8,128)(2,1)S(1)}, u32[]{:S(2)}, u32[]{:S(2)}) collective-permute-start(bf16[400,768]{1,0:T(8,128)(2,1)S(1)} %slice.12.embed), channel_id=1, source_target_pairs={{0,64},{64,0},{128,192},{192,128},{256,320},{320,256},{384,448},{4... | collective-permute-start | bytes 1843208 | tf_op jit(solution)/shard_map/ppermute | solution.py:38
  6.1 1.0 %slice.10.embed_rest = bf16[400,256]{1,0:T(8,128)(2,1)S(1)} slice(f32[400,1024]{1,0:T(8,128)} %bitcast.8), slice={[0:400], [768:1024]} | slice | bytes 409600 | tf_op jit(solution)/shard_map/slice | solution.py:207
  7.1 1.9 %collective-permute-start = (bf16[400,256]{1,0:T(8,128)(2,1)S(1)}, bf16[400,256]{1,0:T(8,128)(2,1)S(1)}, u32[]{:S(2)}, u32[]{:S(2)}) collective-permute-start(bf16[400,256]{1,0:T(8,128)(2,1)S(1)} %slice.10.embed_rest), channel_id=1, source_target_pairs={{0,64},{64,0},{128,192},{192,128},{256,320},{320,256},{384,448},{4... | collective-permute-start | bytes 614408 | tf_op jit(solution)/shard_map/ppermute | solution.py:38
  9.7 0.0 copy-done.6
  9.7 0.0 copy-done.1
  9.7 0.0 copy-done.4
  9.7 0.0 copy-done.5
  9.8 0.0 copy-done.3
  9.8 4.8 %shard_map.103 = (bf16[400,1024]{1,0:T(8,128)(2,1)S(1)}, f32[400,1024]{1,0:T(8,128)S(1)}, bf16[400,1024]{1,0:T(8,128)(2,1)S(1)}, bf16[1024,400]{1,0:T(8,128)(2,1...) custom-call(s32[8]{0:T(128)S(1)} %copy-done.6, s32[1]{0:T(128)S(6)} %copy.11.live, ...), custom_call_target="tpu_custom_call" | custom-call | flops 1677721600 | bytes 8388608 | tf_op jit(solution)/shard_map/pallas_call | solution.py:189
  14.6 0.1 collective-permute-done.1.other
  14.7 2.9 %shard_map.104 = (f32[1024,768]{1,0:T(8,128)S(1)}, f32[1024,1]{1,0:T(8,128)S(1)}, f32[1024,1]{1,0:T(8,128)S(1)}, f32[400,1024]{1,0:T(8,128)S(1)}, f32[400,1024]{1,0:T(8,128)S(1)}) custom-call(bf16[400,768]{1,0:T(8,128)(2,1)S(1)} %collective-permute-done.1.other, bf16[1024,400]{1,0:T(8,128)(2,1)S(1)} %get-tuple-element.31.query_rows, ...), custom_call_target="tpu_custom_call" | custom-call | flops 838860800 | bytes 8388608 | tf_op jit(solution)/shard_map/pallas_call | solution.py:189
  17.7 1.5 %collective-permute-done.rest = bf16[400,256]{1,0:T(8,128)(2,1)S(1)} collective-permute-done((bf16[400,256]{1,0:T(8,128)(2,1)S(1)}, bf16[400,256]{1,0:T(8,128)(2,1)S(1)}, u32[]{:S(2)}, u32[]{:S(2)}) %collective-permute-start) | collective-permute-done | bytes 204832 | tf_op jit(solution)/shard_map/ppermute | solution.py:38
  19.1 2.0 %shard_map.105 = (bf16[1024,1024]{1,0:T(8,128)(2,1)S(1)}, bf16[400,1024]{1,0:T(8,128)(2,1)S(1)}, f32[1,1024]{1,0:T(1,128)S(1)}) custom-call(s32[1]{0:T(128)S(6)} %copy.11.live, bf16[400,256]{1,0:T(8,128)(2,1)S(1)} %collective-permute-done.rest, bf16[400,1024]{1,0:T(8,128)(2,1)S(1)} %get-tuple-element.30.query, ...), custom_call_target="tpu_custom_call" | custom-call | flops 1677721600 | bytes 8388608 | tf_op jit(solution)/shard_map/pallas_call | solution.py:189
  21.2 4.1 %collective-permute-start.2 = (bf16[400,1024]{1,0:T(8,128)(2,1)S(1)}, bf16[400,1024]{1,0:T(8,128)(2,1)S(1)}, u32[]{:S(2)}, u32[]{:S(2)}) collective-permute-start(bf16[400,1024]{1,0:T(8,128)(2,1)S(1)} %get-tuple-element.45), channel_id=1, source_target_pairs={{0,64},{64,0},{128,192},{192,128},{256,320},{320,256},{384,448},{4... | collective-permute-start | bytes 2457608 | tf_op jit(solution)/shard_map/ppermute | solution.py:38
  25.3 1.3 %shard_map.106 = (bf16[400,1024]{1,0:T(8,128)(2,1)S(1)}, bf16[64,8,128]{2,1,0:T(8,128)(2,1)S(1)}) custom-call(bf16[400,256]{1,0:T(8,128)(2,1)S(1)} %collective-permute-done.rest, bf16[1024,1024]{1,0:T(8,128)(2,1)S(1)} %get-tuple-element.38.softmax, bf16[1024,1024]{1,0:T(8,128)(2,1)S(1)} %get-tuple-element.34.target, ...), custom_call_target="tpu_custom_call" | custom-call | flops 1677721600 | bytes 8388608 | tf_op jit(solution)/shard_map/pallas_call | solution.py:189
  26.6 29.2 %all_to_all.10.terms = bf16[64,8,128]{2,1,0:T(8,128)(2,1)S(1)} all-to-all(bf16[64,8,128]{2,1,0:T(8,128)(2,1)S(1)} %get-tuple-element.46), channel_id=1, replica_groups=mesh['y'=8,'x_hi'=2,'x_lo'=2,'z'=8,'core'=2] {'x_hi','x_lo','z','core'}, dimensions={0} | all-to-all | bytes 262144 | tf_op jit(solution)/shard_map/all_to_all | solution.py:42
  55.8 0.7 shard_map.108
  56.5 0.0 copy-start
  56.5 0.0 collective-permute-done.2.received
  56.5 7.0 %all-to-all-start.1 = ((bf16[32,8,128]{2,1,0:T(8,128)(2,1)}), bf16[32,8,128]{2,1,0:T(8,128)(2,1)S(1)}, u32[]{:S(2)}, u32[]{:S(2)}) async-start(bf16[32,8,128]{2,1,0:T(8,128)(2,1)} %shard_map.108), calls=%async_computation.1 | async-start | bytes 131072 | tf_op jit(solution)/shard_map/all_to_all | solution.py:42
  63.5 1.1 %shard_map.107.source_grad = f32[400,1024]{1,0:T(8,128)S(1)} custom-call(bf16[400,1024]{1,0:T(8,128)(2,1)S(1)} %get-tuple-element.44.left_grad, s32[1,1024]{1,0:T(1,128)S(1)} %bitcast.15), custom_call_target="tpu_custom_call" | custom-call | flops 838860800 | bytes 8388608 | tf_op jit(solution)/shard_map/pallas_call | solution.py:189
  64.6 0.0 copy-done
  64.6 0.0 copy-done.2
  64.6 1.7 %shard_map.109 = (f32[400,1024]{1,0:T(8,128)}, f32[1,1024]{1,0:T(1,128)}) custom-call(f32[400,1024]{1,0:T(8,128)S(1)} %bitcast.9, f32[1,1024]{1,0:T(1,128)S(1)} %bitcast.12, f32[400,1024]{1,0:T(8,128)S(1)} %shard_map.107.source_grad, bf16[400,1024]{1,0:T(8,128)(2,1)S(1)} %collective-permute-done.2.received), custom_call_target="tpu_custom_call" | custom-call | flops 8388608 | bytes 8388608 | tf_op jit(solution)/shard_map/pallas_call | solution.py:189
  66.3 5.5 %all-to-all-done.1.terms = bf16[32,8,128]{2,1,0:T(8,128)(2,1)S(1)} async-done(((bf16[32,8,128]{2,1,0:T(8,128)(2,1)}), bf16[32,8,128]{2,1,0:T(8,128)(2,1)S(1)}, u32[]{:S(2)}, u32[]{:S(2)}) %all-to-all-start.1) | async-done | bytes 65568 | tf_op jit(solution)/shard_map/all_to_all | solution.py:42
  71.8 0.6 shard_map.110
  (1 shorter events, 0.0 us)
Async XLA Ops:
  0.6 9.1 %copy-start.6 = (s32[8]{0:T(128)S(1)}, s32[8]{0:T(128)}, u32[]{:S(2)}) copy-start(s32[8]{0:T(128)} %starts.1) | copy-start | bytes 100
  0.6 9.1 %copy-start.1 = (s32[1024]{0:T(1024)S(1)}, s32[1024]{0:T(1024)}, u32[]{:S(2)}) copy-start(s32[1024]{0:T(1024)} %param.13) | copy-start | bytes 12292
  0.7 9.1 %copy-start.4 = (s32[1024]{0:T(1024)S(1)}, s32[1024]{0:T(1024)}, u32[]{:S(2)}) copy-start(s32[1024]{0:T(1024)} %param.12) | copy-start | bytes 12292
  0.7 9.1 %copy-start.5 = (s32[1024]{0:T(1024)S(1)}, s32[1024]{0:T(1024)}, u32[]{:S(2)}) copy-start(s32[1024]{0:T(1024)} %param.11) | copy-start | bytes 12292
  0.7 9.1 %copy-start.3 = (f32[8,400]{1,0:T(8,128)S(1)}, f32[8,400]{1,0:T(8,128)}, u32[]{:S(2)}) copy-start(f32[8,400]{1,0:T(8,128)} %relation.1) | copy-start | bytes 38404
  2.1 12.7 %collective-permute-start.1 = (bf16[400,768]{1,0:T(8,128)(2,1)S(1)}, bf16[400,768]{1,0:T(8,128)(2,1)S(1)}, u32[]{:S(2)}, u32[]{:S(2)}) collective-permute-start(bf16[400,768]{1,0:T(8,128)(2,1)S(1)} %slice.12.embed), channel_id=1, source_target_pairs={{0,64},{64,0},{128,192},{192,128},{256,320},{320,256},{384,448},{4... | collective-permute-start | bytes 1843208 | tf_op jit(solution)/shard_map/ppermute | solution.py:38
  7.1 12.0 %collective-permute-start = (bf16[400,256]{1,0:T(8,128)(2,1)S(1)}, bf16[400,256]{1,0:T(8,128)(2,1)S(1)}, u32[]{:S(2)}, u32[]{:S(2)}) collective-permute-start(bf16[400,256]{1,0:T(8,128)(2,1)S(1)} %slice.10.embed_rest), channel_id=1, source_target_pairs={{0,64},{64,0},{128,192},{192,128},{256,320},{320,256},{384,448},{4... | collective-permute-start | bytes 614408 | tf_op jit(solution)/shard_map/ppermute | solution.py:38
  21.2 35.3 %collective-permute-start.2 = (bf16[400,1024]{1,0:T(8,128)(2,1)S(1)}, bf16[400,1024]{1,0:T(8,128)(2,1)S(1)}, u32[]{:S(2)}, u32[]{:S(2)}) collective-permute-start(bf16[400,1024]{1,0:T(8,128)(2,1)S(1)} %get-tuple-element.45), channel_id=1, source_target_pairs={{0,64},{64,0},{128,192},{192,128},{256,320},{320,256},{384,448},{4... | collective-permute-start | bytes 2457608 | tf_op jit(solution)/shard_map/ppermute | solution.py:38
  56.5 8.1 %copy-start = (f32[1024,400]{0,1:T(8,128)S(1)}, f32[1024,400]{0,1:T(8,128)}, u32[]{:S(2)}) copy-start(f32[1024,400]{0,1:T(8,128)} %param.8) | copy-start | bytes 4915204
  56.5 8.1 %copy-start.2 = (f32[1024]{0:T(1024)S(1)}, f32[1024]{0:T(1024)}, u32[]{:S(2)}) copy-start(f32[1024]{0:T(1024)} %param.9) | copy-start | bytes 12292
  56.5 15.3 %all-to-all-start.1 = ((bf16[32,8,128]{2,1,0:T(8,128)(2,1)}), bf16[32,8,128]{2,1,0:T(8,128)(2,1)S(1)}, u32[]{:S(2)}, u32[]{:S(2)}) async-start(bf16[32,8,128]{2,1,0:T(8,128)(2,1)} %shard_map.108), calls=%async_computation.1 | async-start | bytes 131072 | tf_op jit(solution)/shard_map/all_to_all | solution.py:42
